TPU v7x, 128 devices: a whole 4x4x4 slice. The times are simulated.
128 devices in a mesh: ctxa: 16 (over y_hi, x, core), ctxb: 8 (over y_lo, z).
Axes of the slice: x: 4, y: 4 (y_hi: 2, y_lo: 2; y = y_hi * 2 + y_lo), z: 4, core: 2. Of those that a mesh axis runs over, the one named last changes fastest.
Arguments:
- queries: bfloat16 [16384, 768], P(('ctxa', 'ctxb')), may hold values from -64 to 64
- keys: bfloat16 [16384, 128], P(('ctxa', 'ctxb')), may hold values from -6 to 6
- values: bfloat16 [16384, 128], P(('ctxa', 'ctxb')), may hold values from -6 to 6
- grad_out: bfloat16 [16384, 768], P(('ctxa', 'ctxb')), may hold values from -6 to 6
Outputs:
- attended: bfloat16 [16384, 768], P(('ctxa', 'ctxb'))
- grad_q: bfloat16 [16384, 768], P(('ctxa', 'ctxb'))
- grad_k: bfloat16 [16384, 128], P(('ctxa', 'ctxb'))
- grad_v: bfloat16 [16384, 128], P(('ctxa', 'ctxb'))
All inputs are finite; a program needn't handle non-finite values.
Results may differ from a plain program's by a relative error of at most 0.035.
Values may be sent and summed in bfloat16 or wider, within the bound.
A program may use at most 128 MiB of HBM per device.

v0:
```python
import jax
import jax.numpy as jnp
from jax import lax
from jax.sharding import PartitionSpec as P

MASKED = -1e30


def shards(queries, keys, values, grad_out):
    tok_rows, q_width = queries.shape
    head_size = keys.shape[1]
    head_count = q_width // head_size
    width_a = lax.axis_size("ctxa")
    width_b = lax.axis_size("ctxb")
    index_a = lax.axis_index("ctxa")
    index_b = lax.axis_index("ctxb")
    seq_len = tok_rows * width_a * width_b
    score_scale = head_size ** (-0.5)
    local_rows = jnp.arange(tok_rows, dtype=jnp.int32)
    positions = (index_a * width_b + index_b) * tok_rows + local_rows
    quarter = tok_rows // 4
    sub_count = tok_rows // quarter
    q_heads = queries.reshape(tok_rows, head_count, head_size)
    g_heads = grad_out.reshape(tok_rows, head_count, head_size)
    q_parts = [q_heads[segment * quarter : (segment + 1) * quarter] for segment in range(sub_count)]
    g_parts = [g_heads[segment * quarter : (segment + 1) * quarter] for segment in range(sub_count)]
    pos_parts = [
        positions[segment * quarter : (segment + 1) * quarter] for segment in range(sub_count)
    ]

    def masked_scores(segment, key_rows, first_row):
        key_pos = first_row + jnp.arange(key_rows.shape[0], dtype=jnp.int32)
        visible = key_pos[None, :] <= pos_parts[segment][:, None]
        raw = (
            jnp.einsum(
                "qhd,kd->hqk", q_parts[segment], key_rows, preferred_element_type=jnp.float32
            )
            * score_scale
        )
        return (jnp.where(visible[None], raw, MASKED), visible)

    def forward_piece(carried, key_rows, first_row):
        updated = []
        for segment in range(sub_count):

            def advance(stats_now, segment=segment):
                running_max, running_sum = stats_now
                scores, visible = masked_scores(segment, key_rows, first_row)
                new_max = jnp.maximum(running_max, jnp.max(scores, axis=-1))
                probabilities = jnp.where(visible[None], jnp.exp(scores - new_max[..., None]), 0.0)
                new_sum = jnp.sum(probabilities, axis=-1)
                return (new_max, new_sum)

            def forward_unchanged(stats_now):
                return stats_now

            reaches = pos_parts[segment][-1] >= first_row
            updated.append(lax.cond(reaches, advance, forward_unchanged, carried[segment]))
        return tuple(updated)

    key_block = seq_len // 16
    block_count = seq_len // key_block
    block_ids = jnp.arange(block_count, dtype=jnp.int32)
    empty_stats = tuple(
        (
            (
                jnp.full((head_count, quarter), MASKED, jnp.float32),
                jnp.zeros((head_count, quarter), jnp.float32),
            )
            for segment in range(sub_count)
        )
    )
    final_stats = forward_piece(
        empty_stats, lax.all_gather(keys, ("ctxa", "ctxb"), axis=0, tiled=True), jnp.int32(0)
    )
    whole_k, whole_v = (
        lax.all_gather(keys, ("ctxa", "ctxb"), axis=0, tiled=True),
        lax.all_gather(values, ("ctxa", "ctxb"), axis=0, tiled=True),
    )
    log_parts = [final_part[0] + jnp.log(final_part[1]) for final_part in final_stats]

    def slice_keys(first_row, span_rows):
        return (
            lax.dynamic_slice_in_dim(whole_k, first_row, span_rows, 0),
            lax.dynamic_slice_in_dim(whole_v, first_row, span_rows, 0),
        )

    def output_step(out_now, block_id):
        first_row = block_id * key_block
        key_rows, value_rows = slice_keys(first_row, key_block)
        updated = []
        for segment in range(sub_count):

            def output_contribute(current, segment=segment):
                scores, visible = masked_scores(segment, key_rows, first_row)
                probabilities = jnp.where(
                    visible[None], jnp.exp(scores - log_parts[segment][..., None]), 0.0
                )
                return current + jnp.einsum(
                    "hqk,kd->qhd",
                    probabilities.astype(jnp.bfloat16),
                    value_rows,
                    preferred_element_type=jnp.float32,
                )

            def output_unchanged(current):
                return current

            reaches = pos_parts[segment][-1] >= first_row
            updated.append(lax.cond(reaches, output_contribute, output_unchanged, out_now[segment]))
        return (tuple(updated), None)

    out_empty = tuple(
        (jnp.zeros((quarter, head_count, head_size), jnp.float32) for segment in range(sub_count))
    )
    out_final, _ = lax.scan(output_step, out_empty, block_ids)
    out_parts = [part_sum.astype(jnp.bfloat16) for part_sum in out_final]
    delta_parts = [
        jnp.sum(
            g_parts[segment].astype(jnp.float32) * out_parts[segment].astype(jnp.float32), axis=-1
        ).T
        for segment in range(sub_count)
    ]
    attended = jnp.concatenate(out_parts, axis=0).reshape(tok_rows, q_width)

    def tile_terms(segment, key_rows, value_rows, first_row):
        scores, visible = masked_scores(segment, key_rows, first_row)
        probabilities = jnp.where(
            visible[None], jnp.exp(scores - log_parts[segment][..., None]), 0.0
        )
        dweights = jnp.einsum(
            "qhd,kd->hqk", g_parts[segment], value_rows, preferred_element_type=jnp.float32
        )
        dscores = (
            probabilities * (dweights - delta_parts[segment][..., None]) * score_scale
        ).astype(jnp.bfloat16)
        return (probabilities.astype(jnp.bfloat16), dscores)

    def block_grads(key_rows, value_rows, first_row):
        span_rows = key_rows.shape[0]
        query_terms = []
        key_terms = jnp.zeros((span_rows, 2 * head_size), jnp.float32)
        for segment in range(sub_count):

            def block_contribute(segment=segment):
                weights, dscores = tile_terms(segment, key_rows, value_rows, first_row)
                results = []
                results.append(
                    jnp.einsum("hqk,kd->qhd", dscores, key_rows, preferred_element_type=jnp.float32)
                )
                grad_key_part = jnp.einsum(
                    "hqk,qhd->kd", dscores, q_parts[segment], preferred_element_type=jnp.float32
                )
                grad_value_part = jnp.einsum(
                    "hqk,qhd->kd", weights, g_parts[segment], preferred_element_type=jnp.float32
                )
                results.append(jnp.concatenate([grad_key_part, grad_value_part], axis=1))
                return tuple(results)

            def nothing():
                results = []
                results.append(jnp.zeros((quarter, head_count, head_size), jnp.float32))
                results.append(jnp.zeros((span_rows, 2 * head_size), jnp.float32))
                return tuple(results)

            reaches = pos_parts[segment][-1] >= first_row
            results = lax.cond(reaches, block_contribute, nothing)
            query_terms.append(results[0])
            key_terms = key_terms + results[-1]
        return (query_terms, key_terms)

    dq_empty = tuple(
        (jnp.zeros((quarter, head_count, head_size), jnp.float32) for segment in range(sub_count))
    )

    def grad_step(dq_now, block_id):
        first_row = block_id * key_block
        key_rows, value_rows = slice_keys(first_row, key_block)
        query_terms, key_terms = block_grads(key_rows, value_rows, first_row)
        return (
            tuple((current + addition for current, addition in zip(dq_now, query_terms))),
            key_terms,
        )

    dq_final, kv_blocks = lax.scan(grad_step, dq_empty, block_ids)
    own_kv = lax.psum_scatter(
        kv_blocks.reshape(seq_len, 2 * head_size), ("ctxa", "ctxb"), scatter_dimension=0, tiled=True
    )
    grad_q = jnp.concatenate(dq_final, axis=0).astype(jnp.bfloat16).reshape(tok_rows, q_width)
    return (
        attended,
        grad_q,
        own_kv[:, :head_size].astype(jnp.bfloat16),
        own_kv[:, head_size:].astype(jnp.bfloat16),
    )


def solution(mesh):
    return jax.shard_map(
        shards,
        mesh=mesh,
        in_specs=(
            P(("ctxa", "ctxb"), None),
            P(("ctxa", "ctxb"), None),
            P(("ctxa", "ctxb"), None),
            P(("ctxa", "ctxb"), None),
        ),
        out_specs=(
            P(("ctxa", "ctxb"), None),
            P(("ctxa", "ctxb"), None),
            P(("ctxa", "ctxb"), None),
            P(("ctxa", "ctxb"), None),
        ),
        check_vma=False,
    )
```

profile of v0, /device:TPU:0, one launch (start us, length us, event | category | flops | bytes accessed | tf_op | source)
XLA Modules:
  0.0 2160.0 jit_solution(18205618053862701486)
XLA Ops:
  17.3 300.4 %all-gather.3.cloned.1.call-done = bf16[16384,128]{1,0:T(8,128)(2,1)} async-done(((bf16[128,128]{1,0:T(8,128)(2,1)}), bf16[16384,128]{1,0:T(8,128)(2,1)}) %all-gather.3.cloned.1.call-update) | async-done | bytes 4194320 | tf_op jit(solution)/shard_map/all_gather | solution.py:77
  317.7 9.4 conditional.15
  318.7 4.0 fusion.151
  323.4 3.8 select_reduce_fusion.3
  328.4 9.4 conditional.13
  329.4 4.0 fusion.149
  334.0 3.8 select_reduce_fusion.1
  339.1 9.4 conditional.12
  340.1 4.0 fusion.148
  344.7 3.8 select_reduce_fusion
  349.8 9.5 conditional.14
  350.8 4.0 fusion.150
  355.4 3.8 select_reduce_fusion.2
  360.6 265.9 %all-gather.5.cloned.1.call-done = bf16[16384,128]{1,0:T(8,128)(2,1)} async-done(((bf16[128,128]{1,0:T(8,128)(2,1)}), bf16[16384,128]{1,0:T(8,128)(2,1)}) %all-gather.5.cloned.1.call-update) | async-done | bytes 4194320 | tf_op jit(solution)/shard_map/all_gather | solution.py:78
  626.6 166.2 %while.47 = (s32[]{:T(128)}, f32[32,6,128]{2,0,1:T(8,128)S(1)}, f32[32,6,128]{2,0,1:T(8,128)S(1)}, f32[32,6,128]{2,0,1:T(8,128)S(1)}, f32[32,6,128]{2,0,1:T(8,12...) while((s32[]{:T(128)}, f32[32,6,128]{2,0,1:T(8,128)S(1)}, ...), condition=%wide.region_25.26_spmd, body=%wide.region_16.25_spmd.sunk | while | flops 406818816 | bytes 4427907 | solution.py:116
  636.4 2.0 conditional.28
  638.4 2.0 conditional.29
  642.4 2.0 conditional.31
  794.7 341.0 %while.48 = (s32[]{:T(128)}, f32[32,6,128]{2,0,1:T(8,128)}, f32[32,6,128]{2,0,1:T(8,128)}, f32[32,6,128]{2,0,1:T(8,128)}, f32[32,6,128]{2,0,1:T(8,128)}, /*index...) while((s32[]{:T(128)}, f32[32,6,128]{2,0,1:T(8,128)}, ...), condition=%wide.region_39.40_spmd.clone, body=%wide.region_30.39_spmd.clone.sunk | while | flops 1015877632 | bytes 47226164 | solution.py:185
  805.9 3.9 conditional.32
  809.8 3.9 conditional.33
  814.5 3.9 conditional.34
  819.4 4.8 conditional.35
  1140.1 1011.8 %reduce-scatter.2.cloned.1.call-done = f32[128,256]{1,0:T(8,128)} async-done(((f32[16384,256]{1,0:T(8,128)}), f32[128,256]{1,0:T(8,128)}) %reduce-scatter.2.cloned.1.call-update) | async-done | bytes 131088 | tf_op jit(solution)/shard_map/reduce_scatter | solution.py:186
  (677 shorter events, 457.5 us)
Async XLA Ops:
  7.2 310.6 %all-gather.3.cloned.1.call-start = ((), (), s32[]{:S(2)}) async-start(), calls=%async_computation.1 | async-start | bytes 4227072 | tf_op jit(solution)/shard_map/all_gather | solution.py:77
  7.9 618.6 %all-gather.5.cloned.1.call-start = ((), (), s32[]{:S(2)}) async-start(), calls=%async_computation.2 | async-start | bytes 4227072 | tf_op jit(solution)/shard_map/all_gather | solution.py:78
  8.6 2143.3 %reduce-scatter.2.cloned.1.call-start = ((), (), s32[]{:S(2)}) async-start(), calls=%async_computation.3 | async-start | bytes 16908288 | tf_op jit(solution)/shard_map/reduce_scatter | solution.py:186
  818.4 1.1 copy-start
  841.6 1.1 copy-start
  862.1 1.1 copy-start
  882.5 1.1 copy-start
  903.0 1.1 copy-start
  923.5 1.1 copy-start
  944.0 1.1 copy-start
  964.5 1.1 copy-start
  985.0 1.1 copy-start
  1005.6 1.1 copy-start
  1026.1 1.1 copy-start
  1046.6 1.1 copy-start
  1067.1 1.1 copy-start
  1087.6 1.1 copy-start
  1108.1 1.1 copy-start
  1128.5 1.1 copy-start
  1135.7 0.8 copy-start.4
  1135.7 0.8 copy-start.5
  1135.7 0.9 copy-start.6
  1135.7 3.7 copy-start.2
  1135.7 3.7 copy-start.1
  (1 other events, 0.8 us)
Sparse Core Ops, SparseCore 0:
  9.7 307.9 all-gather.2
  319.4 307.0 all-gather.4
  1135.9 1016.0 reduce-scatter.1
where the time goes:
time: 2180 us; the launch traced here: 2160 us
  waiting for transfers between devices  1580 us (72%)
  local copies, waits for them, and re-layouts  307 us (14%)
  other arithmetic  121 us (6%)
  loops' own time  103 us (5%)
  matrix products  33 us (2%)
    reduce_scatter x1, waiting for transfers between devices, shards(): lax.psum_scatter(kv_blocks.reshape(seq_len, 2 * head_size), ('ctxa', 'ctx...  1010 us
    all_gather x1, waiting for transfers between devices, shards(): lax.all_gather(keys, ('ctxa', 'ctxb'), axis=0, tiled=True)  300 us
    all_gather x1, waiting for transfers between devices, shards(): lax.all_gather(values, ('ctxa', 'ctxb'), axis=0, tiled=True)  266 us
    slice x64, local copies, waits for them, and re-layouts, block_grads(): reaches = pos_parts[segment][-1] >= first_row  80.3 us
    slice x64, local copies, waits for them, and re-layouts, output_step(): reaches = pos_parts[segment][-1] >= first_row  80.2 us
    add x32, other arithmetic, grad_step(): current + addition  50.9 us
    another operation x1, loops' own time, shards(): out_final, _ = lax.scan(output_step, out_empty, block_ids)  50.3 us
    another operation x1, loops' own time, shards(): dq_final, kv_blocks = lax.scan(grad_step, dq_empty, block_ids)  49.8 us
  transfers between devices with their start and end apart: 3, of which 3 were waited for; matrix products, arithmetic and copies ran while one was open for 2% of the time, Pallas kernels for 0%

commit v1 on v0

v1 whole, which is shorter than its diff:
```python
import functools
import math

import jax
import jax.numpy as jnp
from jax import lax
from jax.experimental import pallas as pl
from jax.experimental.pallas import tpu as pltpu
from jax.sharding import PartitionSpec as P

MESH = pl.DeviceIdType.MESH
BF16 = jnp.bfloat16
F32 = jnp.float32

HEADS = 6
D = 128
T = 128
QC = HEADS * T
NS = 32
NZ = 4
CB = 2
CK = CB * T
NCH = NS // CB
MAXP = 36
SCALE = D ** -0.5
C2 = SCALE * math.log2(math.e)
LOW = -1e30


def group_row(s, z, b):
    flip = (b + z) % 2
    return s + flip * (NS - 1 - 2 * s)


def chunks_of(s, z, b):
    seen = group_row(s, z, b) + (b >= z).astype(jnp.int32)
    return (seen + CB - 1) // CB


def base_of(s, z, b):
    total = jnp.int32(0)
    for other in range(NZ):
        total = total + jnp.where(other < b, chunks_of(s, z, jnp.int32(other)), 0)
    return total


def transpose_heads(qg, qgt, b):
    for which in range(2):
        for h in range(HEADS):
            rows = pl.ds(which * QC + h * T, T)
            qgt[b, pl.ds(which * D, D), pl.ds(h * T, T)] = qg[b, rows, :].T


def transpose_kv(kv, kvt, block):
    half = block % CB
    for lane in range(CB):

        @pl.when(half == lane)
        def _():
            for which in range(2):
                kvt[block // CB, pl.ds(which * D, D), pl.ds(lane * T, T)] = kv[
                    block, pl.ds(which * T, T), :
                ].T


def key_rows(kv, c):
    return kv[pl.ds(c * CB, CB), pl.ds(0, T), :].reshape(CK, D)


def value_rows(kv, c):
    return kv[pl.ds(c * CB, CB), pl.ds(T, T), :].reshape(CK, D)


def forward_block(s, z, b, kv, kvt, qgt, scores, probs, out_t, stats):
    count = chunks_of(s, z, b)
    base = base_of(s, z, b)
    q_block = group_row(s, z, b) * NZ + b

    def score(c):
        return jnp.dot(key_rows(kv, c), qgt[b, pl.ds(0, D), :], preferred_element_type=F32)

    def top(x):
        return jnp.max(x.reshape(CK // 8, 8, QC), axis=0)

    def score_step(c, high):
        x = score(c)
        scores[c] = x
        return jnp.maximum(high, top(x))

    def last_step(c, high):
        x = score(c)
        row = lax.broadcasted_iota(jnp.int32, (CK, QC), 0)
        col = lax.broadcasted_iota(jnp.int32, (CK, QC), 1)
        key_pos = ((c * CB + row // T) * NZ + z) * T + row % T
        q_pos = q_block * T + col % T
        x = jnp.where(key_pos <= q_pos, x, LOW)
        scores[c] = x
        return jnp.maximum(high, top(x))

    high = jnp.full((8, QC), LOW, F32)
    high = lax.fori_loop(0, count - 1, score_step, high)
    high = lax.fori_loop(jnp.maximum(count - 1, 0), count, last_step, high)
    row_max = jnp.max(high, axis=0, keepdims=True) * C2

    out_t[b] = jnp.zeros((D, QC), F32)

    def prob_step(c, total):
        p = jnp.exp2(scores[c] * C2 - row_max)
        total = total + jnp.sum(p.reshape(CK // 8, 8, QC), axis=0)
        pb = p.astype(BF16)
        probs[base + c] = pb
        out_t[b] += jnp.dot(kvt[c, pl.ds(D, D), :], pb, preferred_element_type=F32)
        return total

    total = lax.fori_loop(0, count, prob_step, jnp.zeros((8, QC), F32))
    row_sum = jnp.sum(total, axis=0, keepdims=True)
    part_delta = jnp.sum(qgt[b, pl.ds(D, D), :].astype(F32) * out_t[b], axis=0, keepdims=True)
    stats[b, z] = jnp.concatenate(
        [row_max, row_sum, part_delta, jnp.zeros((5, QC), F32)], axis=0
    )


def merge_stats(z, b, stats, coef, delta):
    highs = [stats[b, j, pl.ds(0, 1), :] for j in range(NZ)]
    high = functools.reduce(jnp.maximum, highs)
    facs = [jnp.exp2(x - high) for x in highs]
    total = sum(stats[b, j, pl.ds(1, 1), :] * facs[j] for j in range(NZ))
    inv = 1.0 / total
    coef[b] = jnp.exp2(stats[b, z, pl.ds(0, 1), :] - high) * inv
    delta[b] = sum(stats[b, j, pl.ds(2, 1), :] * facs[j] for j in range(NZ)) * inv
    return [f * inv for f in facs]


def backward_tile(s, z, b, c, kv, kvt, qg, qgt, probs, coef, delta, dq_t, dkv):
    base = base_of(s, z, b)
    dw = jnp.dot(value_rows(kv, c), qgt[b, pl.ds(D, D), :], preferred_element_type=F32)
    w = probs[base + c].astype(F32) * coef[b]
    ds = (w * (dw - delta[b])).astype(BF16)
    wb = w.astype(BF16)
    dkv[:, pl.ds(0, D)] += jnp.dot(ds, qg[b, pl.ds(0, QC), :], preferred_element_type=F32)
    dkv[:, pl.ds(D, D)] += jnp.dot(wb, qg[b, pl.ds(QC, QC), :], preferred_element_type=F32)
    dq_t[b] += jnp.dot(kvt[c, pl.ds(0, D), :], ds, preferred_element_type=F32)


def kernel(
    q_ref, k_ref, v_ref, g_ref,
    att_ref, gq_ref, gk_ref, gv_ref,
    kv, kvt, qg, qgt, scores, probs, out_t, dq_t, stats, coef, delta, dkv,
    kv_out, kv_in, o_out, o_in, dq_out, dq_in,
    kv_send, kv_recv, fwd_send, q_send, q_recv, st_send, st_recv,
    o_send, o_recv, dq_send, dq_recv, dkv_send, dkv_recv,
):
    ia = lax.axis_index("ctxa")
    ib = lax.axis_index("ctxb")
    z = ib % NZ
    s = ia * 2 + ib // NZ

    def device(row, plane):
        return (row // 2, (row % 2) * NZ + plane)

    core = ia % 2
    sibling = s + 2 - 4 * core

    def same_core(i):
        own = (s // 4) * 2 + s % 2
        j = (own + i) % (NS // 2)
        return (j // 2) * 4 + core * 2 + j % 2

    barrier = pltpu.get_barrier_semaphore()

    def greet(i, _):
        pl.semaphore_signal(
            barrier, inc=1, device_id=device((s + i) % NS, z), device_id_type=MESH
        )
        return 0

    lax.fori_loop(1, NS, greet, 0)
    for i in range(1, NZ):
        b = (z + i) % NZ
        pl.semaphore_signal(
            barrier, inc=1, device_id=device(group_row(s, z, b), b), device_id_type=MESH
        )

    kv[s, pl.ds(0, T), :] = k_ref[...]
    kv[s, pl.ds(T, T), :] = v_ref[...]
    for h in range(HEADS):
        qg[z, pl.ds(h * T, T), :] = q_ref[:, pl.ds(h * D, D)]
        qg[z, pl.ds(QC + h * T, T), :] = g_ref[:, pl.ds(h * D, D)]

    pl.semaphore_wait(barrier, NS - 1 + NZ - 1)

    def kv_copy(i):
        return pltpu.make_async_remote_copy(
            src_ref=kv.at[s],
            dst_ref=kv.at[s],
            send_sem=kv_send.at[i],
            recv_sem=kv_recv.at[s],
            device_id=device(same_core(i), z),
            device_id_type=MESH,
        )

    def start_kv(i, _):
        kv_copy(i).start()
        return 0

    lax.fori_loop(1, NS // 2, start_kv, 0)

    def q_copy(i):
        b = (z + i) % NZ
        return pltpu.make_async_remote_copy(
            src_ref=qg.at[z],
            dst_ref=qg.at[z],
            send_sem=q_send.at[i],
            recv_sem=q_recv.at[z],
            device_id=device(group_row(s, z, b), b),
            device_id_type=MESH,
        )

    def start_q(i, _):
        q_copy(i).start()
        return 0

    lax.fori_loop(1, NZ, start_q, 0)
    transpose_heads(qg, qgt, z)

    def wait_block(row):
        pltpu.make_async_remote_copy(
            src_ref=kv.at[row],
            dst_ref=kv.at[row],
            send_sem=kv_send.at[0],
            recv_sem=kv_recv.at[row],
            device_id=device(sibling, z),
            device_id_type=MESH,
        ).wait_recv()

    def pass_copy(i):
        row = same_core(i)
        return pltpu.make_async_remote_copy(
            src_ref=kv.at[row],
            dst_ref=kv.at[row],
            send_sem=fwd_send.at[i],
            recv_sem=kv_recv.at[row],
            device_id=device(sibling, z),
            device_id_type=MESH,
        )

    def pass_step(i, _):
        row = same_core(i)

        @pl.when(i > 0)
        def _():
            wait_block(row)

        pass_copy(i).start()
        transpose_kv(kv, kvt, row)
        return 0

    lax.fori_loop(0, NS // 2, pass_step, 0)

    def other_step(i, _):
        row = same_core(i)
        row = row + 2 - 4 * core
        wait_block(row)
        transpose_kv(kv, kvt, row)
        return 0

    lax.fori_loop(0, NS // 2, other_step, 0)

    def st_copy(b, i):
        p = (z + i) % NZ
        return pltpu.make_async_remote_copy(
            src_ref=stats.at[b, z],
            dst_ref=stats.at[b, z],
            send_sem=st_send.at[b, i],
            recv_sem=st_recv.at[b, z],
            device_id=device(group_row(s, z, p), p),
            device_id_type=MESH,
        )

    def o_copy(b):
        return pltpu.make_async_remote_copy(
            src_ref=o_out.at[b],
            dst_ref=o_in.at[z],
            send_sem=o_send.at[b],
            recv_sem=o_recv.at[z],
            device_id=device(group_row(s, z, b), b),
            device_id_type=MESH,
        )

    def dq_copy(b):
        return pltpu.make_async_remote_copy(
            src_ref=dq_out.at[b],
            dst_ref=dq_in.at[z],
            send_sem=dq_send.at[b],
            recv_sem=dq_recv.at[z],
            device_id=device(group_row(s, z, b), b),
            device_id_type=MESH,
        )

    def forward_step(i, _):
        b = (z + i) % NZ

        @pl.when(i > 0)
        def _():
            pltpu.make_async_remote_copy(
                src_ref=qg.at[b],
                dst_ref=qg.at[b],
                send_sem=q_send.at[0],
                recv_sem=q_recv.at[b],
                device_id=device(group_row(s, z, b), b),
                device_id_type=MESH,
            ).wait_recv()
            transpose_heads(qg, qgt, b)

        forward_block(s, z, b, kv, kvt, qgt, scores, probs, out_t, stats)
        lax.fori_loop(1, NZ, lambda j, _: (st_copy(b, j).start(), 0)[1], 0)

        @pl.when(i > 0)
        def _():
            o_out[b] = out_t[b].astype(BF16)
            o_copy(b).start()

        return 0

    lax.fori_loop(0, NZ, forward_step, 0)

    def wait_stats(b, p):
        pltpu.make_async_remote_copy(
            src_ref=stats.at[b, p],
            dst_ref=stats.at[b, p],
            send_sem=st_send.at[b, 0],
            recv_sem=st_recv.at[b, p],
            device_id=device(group_row(s, z, p), p),
            device_id_type=MESH,
        ).wait_recv()

    def merge_step(b, _):
        lax.fori_loop(1, NZ, lambda j, _: (wait_stats(b, (z + j) % NZ), 0)[1], 0)
        merge_stats(z, b, stats, coef, delta)
        dq_t[b] = jnp.zeros((D, QC), F32)
        return 0

    lax.fori_loop(0, NZ, merge_step, 0)

    def dkv_copy(row):
        return pltpu.make_async_remote_copy(
            src_ref=kv_out.at[row],
            dst_ref=kv_in.at[s],
            send_sem=dkv_send.at[row],
            recv_sem=dkv_recv.at[s],
            device_id=device(row, z),
            device_id_type=MESH,
        )

    def chunk_step(c, _):
        dkv[...] = jnp.zeros((CK, 2 * D), F32)

        def tile_step(b, _):
            count = chunks_of(s, z, b)

            @pl.when(c < count)
            def _():
                backward_tile(
                    s, z, b, c, kv, kvt, qg, qgt, probs, coef, delta, dq_t, dkv
                )

            @pl.when((c == jnp.maximum(count - 1, 0)) & (b != z))
            def _():
                dq_out[b] = dq_t[b].astype(BF16)
                dq_copy(b).start()

            return 0

        lax.fori_loop(0, NZ, tile_step, 0)
        for j in range(CB):
            row = c * CB + j
            kv_out[row, pl.ds(0, T), :] = (dkv[pl.ds(j * T, T), pl.ds(0, D)] * SCALE).astype(BF16)
            kv_out[row, pl.ds(T, T), :] = dkv[pl.ds(j * T, T), pl.ds(D, D)].astype(BF16)

            @pl.when(row != s)
            def _():
                dkv_copy(row).start()

        return 0

    lax.fori_loop(0, NCH, chunk_step, 0)

    def wait_o(b):
        pltpu.make_async_remote_copy(
            src_ref=o_out.at[b],
            dst_ref=o_in.at[b],
            send_sem=o_send.at[z],
            recv_sem=o_recv.at[b],
            device_id=device(group_row(s, z, b), b),
            device_id_type=MESH,
        ).wait_recv()

    def wait_dq(b):
        pltpu.make_async_remote_copy(
            src_ref=dq_out.at[b],
            dst_ref=dq_in.at[b],
            send_sem=dq_send.at[z],
            recv_sem=dq_recv.at[b],
            device_id=device(group_row(s, z, b), b),
            device_id_type=MESH,
        ).wait_recv()

    highs = [stats[z, j, pl.ds(0, 1), :] for j in range(NZ)]
    high = functools.reduce(jnp.maximum, highs)
    total = sum(stats[z, j, pl.ds(1, 1), :] * jnp.exp2(highs[j] - high) for j in range(NZ))
    out_t[z] = out_t[z] * coef[z]

    def add_o(i, _):
        b = (z + i) % NZ
        wait_o(b)
        fac = jnp.exp2(stats[z, b, pl.ds(0, 1), :] - high) / total
        out_t[z] += o_in[b].astype(F32) * fac
        return 0

    lax.fori_loop(1, NZ, add_o, 0)
    for h in range(HEADS):
        att_ref[:, pl.ds(h * D, D)] = out_t[z, :, pl.ds(h * T, T)].T.astype(BF16)

    def add_dq(i, _):
        b = (z + i) % NZ
        wait_dq(b)
        dq_t[z] += dq_in[b].astype(F32)
        return 0

    lax.fori_loop(1, NZ, add_dq, 0)
    for h in range(HEADS):
        gq_ref[:, pl.ds(h * D, D)] = (dq_t[z, :, pl.ds(h * T, T)] * SCALE).T.astype(BF16)

    dkv[:, pl.ds(0, D)] = kv_out[s].astype(F32)

    def add_kv(i, _):
        row = (s + i) % NS
        pltpu.make_async_remote_copy(
            src_ref=kv_out.at[row],
            dst_ref=kv_in.at[row],
            send_sem=dkv_send.at[s],
            recv_sem=dkv_recv.at[row],
            device_id=device(row, z),
            device_id_type=MESH,
        ).wait_recv()
        dkv[:, pl.ds(0, D)] += kv_in[row].astype(F32)
        return 0

    lax.fori_loop(1, NS, add_kv, 0)
    gk_ref[...] = dkv[pl.ds(0, T), pl.ds(0, D)].astype(BF16)
    gv_ref[...] = dkv[pl.ds(T, T), pl.ds(0, D)].astype(BF16)

    lax.fori_loop(1, NS // 2, lambda i, _: (kv_copy(i).wait_send(), 0)[1], 0)
    lax.fori_loop(0, NS // 2, lambda i, _: (pass_copy(i).wait_send(), 0)[1], 0)
    lax.fori_loop(1, NZ, lambda i, _: (q_copy(i).wait_send(), 0)[1], 0)

    def drain_group(i, _):
        b = (z + i) % NZ
        o_copy(b).wait_send()
        dq_copy(b).wait_send()
        return 0

    lax.fori_loop(1, NZ, drain_group, 0)

    def drain_stats(b, _):
        lax.fori_loop(1, NZ, lambda j, _: (st_copy(b, j).wait_send(), 0)[1], 0)
        return 0

    lax.fori_loop(0, NZ, drain_stats, 0)
    lax.fori_loop(1, NS, lambda i, _: (dkv_copy((s + i) % NS).wait_send(), 0)[1], 0)


def shards(queries, keys, values, grad_out):
    vmem = pl.BlockSpec(memory_space=pltpu.VMEM)
    dma = pltpu.SemaphoreType.DMA
    return pl.pallas_call(
        kernel,
        out_shape=(
            jax.ShapeDtypeStruct((T, QC), BF16),
            jax.ShapeDtypeStruct((T, QC), BF16),
            jax.ShapeDtypeStruct((T, D), BF16),
            jax.ShapeDtypeStruct((T, D), BF16),
        ),
        in_specs=[vmem] * 4,
        out_specs=(vmem,) * 4,
        scratch_shapes=[
            pltpu.VMEM((NS, 2 * T, D), BF16),
            pltpu.VMEM((NCH, 2 * D, CK), BF16),
            pltpu.VMEM((NZ, 2 * QC, D), BF16),
            pltpu.VMEM((NZ, 2 * D, QC), BF16),
            pltpu.VMEM((NCH, CK, QC), F32),
            pltpu.VMEM((MAXP, CK, QC), BF16),
            pltpu.VMEM((NZ, D, QC), F32),
            pltpu.VMEM((NZ, D, QC), F32),
            pltpu.VMEM((NZ, NZ, 8, QC), F32),
            pltpu.VMEM((NZ, 1, QC), F32),
            pltpu.VMEM((NZ, 1, QC), F32),
            pltpu.VMEM((CK, 2 * D), F32),
            pltpu.VMEM((NS, 2 * T, D), BF16),
            pltpu.VMEM((NS, 2 * T, D), BF16),
            pltpu.VMEM((NZ, D, QC), BF16),
            pltpu.VMEM((NZ, D, QC), BF16),
            pltpu.VMEM((NZ, D, QC), BF16),
            pltpu.VMEM((NZ, D, QC), BF16),
            dma((NS // 2,)),
            dma((NS,)),
            dma((NS // 2,)),
            dma((NZ,)),
            dma((NZ,)),
            dma((NZ, NZ)),
            dma((NZ, NZ)),
            dma((NZ,)),
            dma((NZ,)),
            dma((NZ,)),
            dma((NZ,)),
            dma((NS,)),
            dma((NS,)),
        ],
        compiler_params=pltpu.CompilerParams(
            collective_id=0, has_side_effects=True, vmem_limit_bytes=60 * 1024 * 1024
        ),
        cost_estimate=pl.CostEstimate(
            flops=10_000_000_000, bytes_accessed=10_000_000, transcendentals=6_500_000
        ),
    )(queries, keys, values, grad_out)


def solution(mesh):
    spec = P(("ctxa", "ctxb"), None)
    return jax.shard_map(
        shards,
        mesh=mesh,
        in_specs=(spec,) * 4,
        out_specs=(spec,) * 4,
        check_vma=False,
    )
```

time: 2180 us -> 124 us (0.06)
  the two profiles are of different devices: /device:TPU:0 before, /device:TPU:55 now
where the time goes in v1:
time: 124 us
  Pallas kernels  119 us (96%)
  local copies, waits for them, and re-layouts  3.8 us (3%)
    pallas_call x1, Pallas kernels, shards(): pl.pallas_call(kernel, out_shape=(jax.ShapeDtypeStruct((T, QC), BF16), ja...  119 us
    unnamed x10, local copies, waits for them, and re-layouts  3.8 us

profile of v1, /device:TPU:55, one launch (start us, length us, event | category | flops | bytes accessed | tf_op | source)
XLA Modules:
  0.0 123.9 jit_solution(17010571327667071896)
XLA Ops:
  0.6 119.5 %shard_map.75 = (bf16[128,768]{1,0:T(8,128)(2,1)}, bf16[128,768]{1,0:T(8,128)(2,1)}, bf16[128,128]{1,0:T(8,128)(2,1)}, bf16[128,128]{1,0:T(8,128)(2,1)}) custom-call(bf16[128,768]{1,0:T(8,128)(2,1)} %q_ref.1, bf16[128,128]{1,0:T(8,128)(2,1)} %k_ref.1, bf16[128,128]{1,0:T(8,128)(2,1)} %v_ref.1, bf16[128,768]{1,0:T(8,128)(2,1)} %g_ref.1), custom_call_target="tpu_custom_call" | custom-call | flops 10000000000 | bytes 10000000 | tf_op jit(solution)/shard_map/pallas_call | solution.py:476
  120.1 0.0 copy-start
  120.1 1.7 %copy.12 = bf16[128,768]{1,0:T(8,128)(2,1)} copy(bf16[128,768]{1,0:T(8,128)(2,1)} %get-tuple-element.8) | data formatting | bytes 393216
  121.8 0.0 copy-done
  121.8 0.0 copy-start.2
  121.8 0.7 copy.13
  122.4 0.1 copy-done.2
  122.5 0.0 copy-start.1
  122.5 0.6 copy.14
  123.1 0.2 copy-done.1
  123.3 0.6 copy.15
Async XLA Ops:
  120.1 1.7 %copy-start = (bf16[128,768]{1,0:T(8,128)(2,1)S(1)}, bf16[128,768]{1,0:T(8,128)(2,1)}, u32[]{:S(2)}) copy-start(bf16[128,768]{1,0:T(8,128)(2,1)} %get-tuple-element.9) | copy-start | bytes 589828
  121.8 0.8 copy-start.2
  122.5 0.8 copy-start.1

commit v2 on v1

v2 whole, which is shorter than its diff:
```python
import functools
import math

import jax
import jax.numpy as jnp
from jax import lax
from jax.experimental import pallas as pl
from jax.experimental.pallas import tpu as pltpu
from jax.sharding import PartitionSpec as P

MESH = pl.DeviceIdType.MESH
BF16 = jnp.bfloat16
F32 = jnp.float32

HEADS = 6
D = 128
T = 128
QC = HEADS * T
NS = 32
NZ = 4
CB = 2
CK = CB * T
NCH = NS // CB
MAXP = 36
SCALE = D ** -0.5
C2 = SCALE * math.log2(math.e)
LOW = -1e30


def group_row(s, z, b):
    flip = (b + z) % 2
    return s + flip * (NS - 1 - 2 * s)


def chunks_of(s, z, b):
    seen = group_row(s, z, b) + (b >= z).astype(jnp.int32)
    return (seen + CB - 1) // CB


def base_of(s, z, b):
    total = jnp.int32(0)
    for other in range(NZ):
        total = total + jnp.where(other < b, chunks_of(s, z, jnp.int32(other)), 0)
    return total


def transpose_heads(src, dst, b):
    for h in range(HEADS):
        dst[b, :, pl.ds(h * T, T)] = src[b, pl.ds(h * T, T), :].T


def transpose_rows(src, dst, row):
    for lane in range(CB):

        @pl.when(row % CB == lane)
        def _():
            dst[row // CB, :, pl.ds(lane * T, T)] = src[row].T


def chunk_rows(src, c):
    return src[pl.ds(c * CB, CB)].reshape(CK, D)


def score_block(s, z, b, kb, qt, scores):
    count = chunks_of(s, z, b)
    q_block = group_row(s, z, b) * NZ + b

    def score(c):
        return jnp.dot(chunk_rows(kb, c), qt[b], preferred_element_type=F32)

    def top(x):
        return jnp.max(x.reshape(CK // 8, 8, QC), axis=0)

    def score_step(c, high):
        x = score(c)
        scores[c] = x
        return jnp.maximum(high, top(x))

    def last_step(c, high):
        x = score(c)
        row = lax.broadcasted_iota(jnp.int32, (CK, QC), 0)
        col = lax.broadcasted_iota(jnp.int32, (CK, QC), 1)
        key_pos = ((c * CB + row // T) * NZ + z) * T + row % T
        q_pos = q_block * T + col % T
        x = jnp.where(key_pos <= q_pos, x, LOW)
        scores[c] = x
        return jnp.maximum(high, top(x))

    high = jnp.full((8, QC), LOW, F32)
    high = lax.fori_loop(0, count - 1, score_step, high)
    high = lax.fori_loop(jnp.maximum(count - 1, 0), count, last_step, high)
    return jnp.max(high, axis=0, keepdims=True) * C2


def prob_block(s, z, b, row_max, vt, scores, probs, out_t):
    count = chunks_of(s, z, b)
    base = base_of(s, z, b)
    out_t[b] = jnp.zeros((D, QC), F32)

    def prob_step(c, total):
        p = jnp.exp2(scores[c] * C2 - row_max)
        total = total + jnp.sum(p.reshape(CK // 8, 8, QC), axis=0)
        pb = p.astype(BF16)
        probs[base + c] = pb
        out_t[b] += jnp.dot(vt[c], pb, preferred_element_type=F32)
        return total

    total = lax.fori_loop(0, count, prob_step, jnp.zeros((8, QC), F32))
    return jnp.sum(total, axis=0, keepdims=True)


def stat_block(z, b, row_max, row_sum, gt, out_t, stats):
    part_delta = jnp.sum(gt[b].astype(F32) * out_t[b], axis=0, keepdims=True)
    stats[b, z] = jnp.concatenate(
        [row_max, row_sum, part_delta, jnp.zeros((5, QC), F32)], axis=0
    )


def merge_stats(z, b, stats, coef, delta):
    highs = [stats[b, j, pl.ds(0, 1), :] for j in range(NZ)]
    high = functools.reduce(jnp.maximum, highs)
    facs = [jnp.exp2(x - high) for x in highs]
    total = sum(stats[b, j, pl.ds(1, 1), :] * facs[j] for j in range(NZ))
    inv = 1.0 / total
    coef[b] = jnp.exp2(stats[b, z, pl.ds(0, 1), :] - high) * inv
    delta[b] = sum(stats[b, j, pl.ds(2, 1), :] * facs[j] for j in range(NZ)) * inv


def backward_tile(s, z, b, c, vb, kt, qh, gh, gt, probs, coef, delta, dq_t, dkv):
    base = base_of(s, z, b)
    dw = jnp.dot(chunk_rows(vb, c), gt[b], preferred_element_type=F32)
    w = probs[base + c].astype(F32) * coef[b]
    ds = (w * (dw - delta[b])).astype(BF16)
    wb = w.astype(BF16)
    dkv[c, :, pl.ds(0, D)] += jnp.dot(ds, qh[b], preferred_element_type=F32)
    dkv[c, :, pl.ds(D, D)] += jnp.dot(wb, gh[b], preferred_element_type=F32)
    dq_t[b] += jnp.dot(kt[c], ds, preferred_element_type=F32)


def kernel(
    q_ref, k_ref, v_ref, g_ref,
    att_ref, gq_ref, gk_ref, gv_ref,
    kb, vb, kt, vt, qh, gh, qt, gt, scores, probs, out_t, dq_t, stats, coef, delta, dkv,
    sib_in, kv_out, kv_in, o_out, o_in, dq_out, dq_in,
    k_send, k_recv, kf_send, v_send, v_recv, vf_send, q_send, q_recv, g_send, g_recv,
    st_send, st_recv, o_send, o_recv, dq_send, dq_recv, sib_send, sib_recv, dkv_send, dkv_recv,
):
    ia = lax.axis_index("ctxa")
    ib = lax.axis_index("ctxb")
    z = ib % NZ
    s = ia * 2 + ib // NZ
    core = ia % 2
    x = (ia // 2) % 4
    y = (ia // 8) * 2 + ib // NZ
    sibling = s + 2 - 4 * core
    chip = (s // 4) * 2 + s % 2

    def device(row, plane):
        return (row // 2, (row % 2) * NZ + plane)

    def remote(src, dst, send, recv, row, plane):
        return pltpu.make_async_remote_copy(
            src_ref=src, dst_ref=dst, send_sem=send, recv_sem=recv,
            device_id=device(row, plane), device_id_type=MESH,
        )

    def each(low, high, step):
        lax.fori_loop(low, high, lambda i, _: (step(i), 0)[1], 0)

    def moved(i, sign):
        nx = (x + sign * (i % 4) + 4) % 4
        ny = (y + sign * (i // 4) + 4) % 4
        return (ny // 2) * 16 + nx * 4 + core * 2 + ny % 2

    def member(i):
        b = (z + i) % NZ
        return b, group_row(s, z, b)

    barrier = pltpu.get_barrier_semaphore()

    def signal(row, plane):
        pl.semaphore_signal(
            barrier, inc=1, device_id=device(row, plane), device_id_type=MESH
        )

    each(1, NS, lambda i: signal((s + i) % NS, z))
    for i in range(1, NZ):
        b, row = member(i)
        signal(row, b)

    kb[s] = k_ref[...]
    vb[s] = v_ref[...]
    for h in range(HEADS):
        qh[z, pl.ds(h * T, T), :] = q_ref[:, pl.ds(h * D, D)]
        gh[z, pl.ds(h * T, T), :] = g_ref[:, pl.ds(h * D, D)]

    pl.semaphore_wait(barrier, NS - 1 + NZ - 1)

    def k_copy(i):
        return remote(kb.at[s], kb.at[s], k_send.at[i], k_recv.at[s], moved(i, 1), z)

    def v_copy(i):
        return remote(vb.at[s], vb.at[s], v_send.at[i], v_recv.at[s], moved(i, 1), z)

    def q_copy(i):
        b, row = member(i)
        return remote(qh.at[z], qh.at[z], q_send.at[i], q_recv.at[z], row, b)

    def g_copy(i):
        b, row = member(i)
        return remote(gh.at[z], gh.at[z], g_send.at[i], g_recv.at[z], row, b)

    def k_pass(i):
        row = moved(i, -1)
        return remote(kb.at[row], kb.at[row], kf_send.at[i], k_recv.at[row], sibling, z)

    def v_pass(i):
        row = moved(i, -1)
        return remote(vb.at[row], vb.at[row], vf_send.at[i], v_recv.at[row], sibling, z)

    q_copy(2).start()
    each(1, NS // 2, lambda i: k_copy(i).start())
    q_copy(1).start()
    q_copy(3).start()
    each(1, NS // 2, lambda i: v_copy(i).start())
    each(1, NZ, lambda i: g_copy(i).start())

    transpose_heads(qh, qt, z)
    transpose_heads(gh, gt, z)
    dkv[...] = jnp.zeros((NCH, CK, 2 * D), F32)
    dq_t[...] = jnp.zeros((NZ, D, QC), F32)

    def gather(buf, flipped, copy, send, recv):
        def wait(row):
            remote(buf.at[row], buf.at[row], send.at[0], recv.at[row], sibling, z).wait_recv()

        def near(i):
            row = moved(i, -1)

            @pl.when(i > 0)
            def _():
                wait(row)

            copy(i).start()
            transpose_rows(buf, flipped, row)

        def far(i):
            row = moved(i, -1) + 2 - 4 * core
            wait(row)
            transpose_rows(buf, flipped, row)

        each(0, NS // 2, near)
        each(0, NS // 2, far)

    gather(kb, kt, k_pass, k_send, k_recv)

    def st_copy(b, i):
        p, row = member(i)
        return remote(stats.at[b, z], stats.at[b, z], st_send.at[b, i], st_recv.at[b, z], row, p)

    def o_copy(b):
        return remote(
            o_out.at[b], o_in.at[z], o_send.at[b], o_recv.at[z], group_row(s, z, b), b
        )

    def dq_copy(b):
        return remote(
            dq_out.at[b], dq_in.at[z], dq_send.at[b], dq_recv.at[z], group_row(s, z, b), b
        )

    def forward_step(i):
        b = (z + i + (i == 2).astype(jnp.int32) - (i == 3).astype(jnp.int32)) % NZ
        row = group_row(s, z, b)

        @pl.when(i > 0)
        def _():
            remote(qh.at[b], qh.at[b], q_send.at[0], q_recv.at[b], row, b).wait_recv()
            transpose_heads(qh, qt, b)

        row_max = score_block(s, z, b, kb, qt, scores)

        @pl.when(i == 0)
        def _():
            gather(vb, vt, v_pass, v_send, v_recv)

        row_sum = prob_block(s, z, b, row_max, vt, scores, probs, out_t)

        @pl.when(i > 0)
        def _():
            o_out[b] = out_t[b].astype(BF16)
            o_copy(b).start()
            remote(gh.at[b], gh.at[b], g_send.at[0], g_recv.at[b], row, b).wait_recv()
            transpose_heads(gh, gt, b)

        stat_block(z, b, row_max, row_sum, gt, out_t, stats)
        each(1, NZ, lambda j: st_copy(b, j).start())

    each(0, NZ, forward_step)

    def merge(b):
        def wait(j):
            p, row = member(j)
            remote(
                stats.at[b, p], stats.at[b, p], st_send.at[b, 0], st_recv.at[b, p], row, p
            ).wait_recv()

        each(1, NZ, wait)
        merge_stats(z, b, stats, coef, delta)

    def tile(b, c):
        backward_tile(s, z, b, c, vb, kt, qh, gh, gt, probs, coef, delta, dq_t, dkv)

    def send_dq(b):
        dq_out[b] = dq_t[b].astype(BF16)
        dq_copy(b).start()

    def first_group(i):
        b = (z + 1 + 2 * i) % NZ
        merge(b)
        each(0, chunks_of(s, z, b), lambda c: tile(b, c))
        send_dq(b)

    each(0, 2, first_group)
    merge((z + 2) % NZ)
    merge(z)

    def chunk_at(i):
        ny = (y // 2 + i // 8) % 2
        nx = (x + (i // 2) % 4) % 4
        return ny * 8 + nx * 2 + i % 2

    def sib_copy(i):
        c = chunk_at(i)
        return remote(
            dkv.at[c, pl.ds((1 - core) * T, T), :], sib_in.at[i], sib_send.at[i], sib_recv.at[i], sibling, z
        )

    def dkv_copy(i):
        row = chunk_at(i) * CB + core
        return remote(kv_out.at[i], kv_in.at[chip], dkv_send.at[i], dkv_recv.at[chip], row, z)

    def finish(i):
        c = chunk_at(i)
        sib_copy(i).wait_recv()
        terms = dkv[c, pl.ds(core * T, T), :] + sib_in[i]
        kv_out[i, pl.ds(0, T), :] = (terms[:, :D] * SCALE).astype(BF16)
        kv_out[i, pl.ds(T, T), :] = terms[:, D:].astype(BF16)

        @pl.when(c * CB + core != s)
        def _():
            dkv_copy(i).start()

        @pl.when(c * CB + core == s)
        def _():
            kv_in[chip] = kv_out[i]

    def chunk_step(i):
        c = chunk_at(i)

        def one(j):
            b = (z + 2 * j) % NZ

            @pl.when(c < chunks_of(s, z, b))
            def _():
                tile(b, c)

        each(0, 2, one)
        sib_copy(i).start()

        @pl.when(i > 0)
        def _():
            finish(i - 1)

    each(0, NCH, chunk_step)
    send_dq((z + 2) % NZ)
    finish(NCH - 1)

    highs = [stats[z, j, pl.ds(0, 1), :] for j in range(NZ)]
    high = functools.reduce(jnp.maximum, highs)
    total = sum(stats[z, j, pl.ds(1, 1), :] * jnp.exp2(highs[j] - high) for j in range(NZ))
    out_t[z] = out_t[z] * coef[z]

    def add_o(i):
        b, row = member(i)
        remote(o_out.at[b], o_in.at[b], o_send.at[z], o_recv.at[b], row, b).wait_recv()
        fac = jnp.exp2(stats[z, b, pl.ds(0, 1), :] - high) / total
        out_t[z] += o_in[b].astype(F32) * fac

    each(1, NZ, add_o)
    for h in range(HEADS):
        att_ref[:, pl.ds(h * D, D)] = out_t[z, :, pl.ds(h * T, T)].T.astype(BF16)

    def add_dq(i):
        b, row = member(i)
        remote(dq_out.at[b], dq_in.at[b], dq_send.at[z], dq_recv.at[b], row, b).wait_recv()
        dq_t[z] += dq_in[b].astype(F32)

    each(1, NZ, add_dq)
    for h in range(HEADS):
        gq_ref[:, pl.ds(h * D, D)] = (dq_t[z, :, pl.ds(h * T, T)] * SCALE).T.astype(BF16)

    def add_kv(i, total):
        other = (i // 2) * 4 + (s % 2) * 2 + i % 2

        @pl.when(other != s)
        def _():
            remote(
                kv_out.at[0], kv_in.at[i], dkv_send.at[0], dkv_recv.at[i], other, z
            ).wait_recv()

        return total + kv_in[i].astype(F32)

    total = lax.fori_loop(0, NS // 2, add_kv, jnp.zeros((2 * T, D), F32))
    gk_ref[...] = total[:T].astype(BF16)
    gv_ref[...] = total[T:].astype(BF16)

    each(1, NS // 2, lambda i: k_copy(i).wait_send())
    each(1, NS // 2, lambda i: v_copy(i).wait_send())
    each(0, NS // 2, lambda i: k_pass(i).wait_send())
    each(0, NS // 2, lambda i: v_pass(i).wait_send())

    def drain_group(i):
        b, _ = member(i)
        q_copy(i).wait_send()
        g_copy(i).wait_send()
        o_copy(b).wait_send()
        dq_copy(b).wait_send()

    each(1, NZ, drain_group)
    each(0, NZ, lambda b: each(1, NZ, lambda j: st_copy(b, j).wait_send()))

    def drain_kv(i):
        sib_copy(i).wait_send()

        @pl.when(chunk_at(i) * CB + core != s)
        def _():
            dkv_copy(i).wait_send()

    each(0, NCH, drain_kv)


def shards(queries, keys, values, grad_out):
    vmem = pl.BlockSpec(memory_space=pltpu.VMEM)
    dma = pltpu.SemaphoreType.DMA
    return pl.pallas_call(
        kernel,
        out_shape=(
            jax.ShapeDtypeStruct((T, QC), BF16),
            jax.ShapeDtypeStruct((T, QC), BF16),
            jax.ShapeDtypeStruct((T, D), BF16),
            jax.ShapeDtypeStruct((T, D), BF16),
        ),
        in_specs=[vmem] * 4,
        out_specs=(vmem,) * 4,
        scratch_shapes=[
            pltpu.VMEM((NS, T, D), BF16),
            pltpu.VMEM((NS, T, D), BF16),
            pltpu.VMEM((NCH, D, CK), BF16),
            pltpu.VMEM((NCH, D, CK), BF16),
            pltpu.VMEM((NZ, QC, D), BF16),
            pltpu.VMEM((NZ, QC, D), BF16),
            pltpu.VMEM((NZ, D, QC), BF16),
            pltpu.VMEM((NZ, D, QC), BF16),
            pltpu.VMEM((NCH, CK, QC), F32),
            pltpu.VMEM((MAXP, CK, QC), BF16),
            pltpu.VMEM((NZ, D, QC), F32),
            pltpu.VMEM((NZ, D, QC), F32),
            pltpu.VMEM((NZ, NZ, 8, QC), F32),
            pltpu.VMEM((NZ, 1, QC), F32),
            pltpu.VMEM((NZ, 1, QC), F32),
            pltpu.VMEM((NCH, CK, 2 * D), F32),
            pltpu.VMEM((NCH, T, 2 * D), F32),
            pltpu.VMEM((NCH, 2 * T, D), BF16),
            pltpu.VMEM((NS // 2, 2 * T, D), BF16),
            pltpu.VMEM((NZ, D, QC), BF16),
            pltpu.VMEM((NZ, D, QC), BF16),
            pltpu.VMEM((NZ, D, QC), BF16),
            pltpu.VMEM((NZ, D, QC), BF16),
            dma((NS // 2,)),
            dma((NS,)),
            dma((NS // 2,)),
            dma((NS // 2,)),
            dma((NS,)),
            dma((NS // 2,)),
            dma((NZ,)),
            dma((NZ,)),
            dma((NZ,)),
            dma((NZ,)),
            dma((NZ, NZ)),
            dma((NZ, NZ)),
            dma((NZ,)),
            dma((NZ,)),
            dma((NZ,)),
            dma((NZ,)),
            dma((NCH,)),
            dma((NCH,)),
            dma((NCH,)),
            dma((NS // 2,)),
        ],
        compiler_params=pltpu.CompilerParams(
            collective_id=0, has_side_effects=True, vmem_limit_bytes=60 * 1024 * 1024
        ),
        cost_estimate=pl.CostEstimate(
            flops=10_000_000_000, bytes_accessed=10_000_000, transcendentals=6_500_000
        ),
    )(queries, keys, values, grad_out)


def solution(mesh):
    spec = P(("ctxa", "ctxb"), None)
    return jax.shard_map(
        shards,
        mesh=mesh,
        in_specs=(spec,) * 4,
        out_specs=(spec,) * 4,
        check_vma=False,
    )
```

time: 124 us -> 104 us (0.84)
  the two profiles are of different devices: /device:TPU:55 before, /device:TPU:0 now
where the time goes in v2:
time: 104 us; the launch traced here: 102 us
  Pallas kernels  97.6 us (94%)
  local copies, waits for them, and re-layouts  3.8 us (4%)
    pallas_call x1, Pallas kernels, shards(): pl.pallas_call(kernel, out_shape=(jax.ShapeDtypeStruct((T, QC), BF16), ja...  97.6 us
    unnamed x10, local copies, waits for them, and re-layouts  3.8 us

profile of v2, /device:TPU:0, one launch (start us, length us, event | category | flops | bytes accessed | tf_op | source)
XLA Modules:
  0.0 102.0 jit_solution(5819119554283495390)
XLA Ops:
  0.6 97.6 %shard_map.75 = (bf16[128,768]{1,0:T(8,128)(2,1)}, bf16[128,768]{1,0:T(8,128)(2,1)}, bf16[128,128]{1,0:T(8,128)(2,1)}, bf16[128,128]{1,0:T(8,128)(2,1)}) custom-call(bf16[128,768]{1,0:T(8,128)(2,1)} %q_ref.1, bf16[128,128]{1,0:T(8,128)(2,1)} %k_ref.1, bf16[128,128]{1,0:T(8,128)(2,1)} %v_ref.1, bf16[128,768]{1,0:T(8,128)(2,1)} %g_ref.1), custom_call_target="tpu_custom_call" | custom-call | flops 10000000000 | bytes 10000000 | tf_op jit(solution)/shard_map/pallas_call | solution.py:445
  98.2 0.0 copy-start
  98.2 1.7 %copy.12 = bf16[128,768]{1,0:T(8,128)(2,1)} copy(bf16[128,768]{1,0:T(8,128)(2,1)} %get-tuple-element.8) | data formatting | bytes 393216
  99.9 0.0 copy-done
  99.9 0.0 copy-start.2
  99.9 0.7 copy.13
  100.6 0.1 copy-done.2
  100.7 0.0 copy-start.1
  100.7 0.6 copy.14
  101.3 0.2 copy-done.1
  101.4 0.6 copy.15
Async XLA Ops:
  98.2 1.7 %copy-start = (bf16[128,768]{1,0:T(8,128)(2,1)S(1)}, bf16[128,768]{1,0:T(8,128)(2,1)}, u32[]{:S(2)}) copy-start(bf16[128,768]{1,0:T(8,128)(2,1)} %get-tuple-element.9) | copy-start | bytes 589828
  99.9 0.8 copy-start.2
  100.7 0.8 copy-start.1

commit v3 on v2

v3 whole, which is shorter than its diff:
```python
import functools
import math

import jax
import jax.numpy as jnp
from jax import lax
from jax.experimental import pallas as pl
from jax.experimental.pallas import tpu as pltpu
from jax.sharding import PartitionSpec as P

MESH = pl.DeviceIdType.MESH
BF16 = jnp.bfloat16
F32 = jnp.float32

HEADS = 6
D = 128
T = 128
QC = HEADS * T
NS = 32
NZ = 4
CB = 2
CK = CB * T
NCH = NS // CB
ROUNDS = NS // 4
MAXP = 36
SCALE = D ** -0.5
C2 = SCALE * math.log2(math.e)
LOW = -1e30


def group_row(s, z, b):
    flip = (b + z) % 2
    return s + flip * (NS - 1 - 2 * s)


def chunks_of(s, z, b):
    seen = group_row(s, z, b) + (b >= z).astype(jnp.int32)
    return (seen + CB - 1) // CB


def base_of(s, z, b):
    total = jnp.int32(0)
    for other in range(NZ):
        total = total + jnp.where(other < b, chunks_of(s, z, jnp.int32(other)), 0)
    return total


def transpose_heads(src, dst, b):
    for h in range(HEADS):
        dst[b, :, pl.ds(h * T, T)] = src[b, pl.ds(h * T, T), :].T


def transpose_rows(src, dst, row):
    dst[:, pl.ds(pl.multiple_of(row * T, T), T)] = src[row].T


def rows_of(src, c, size):
    return src[pl.ds(c * CB, size * CB)].reshape(size * CK, D)


def lanes_of(src, c, size):
    return src[:, pl.ds(pl.multiple_of(c * CK, CK), size * CK)]


def tiles(count, step, carry):
    big = count // 4
    carry = lax.fori_loop(0, big, lambda i, now: step(4 * i, 4, now), carry)
    carry = lax.fori_loop(0, (count % 4) // 2, lambda i, now: step(4 * big, 2, now), carry)
    return lax.fori_loop(0, count % 2, lambda i, now: step(count - 1, 1, now), carry)


def score_block(s, z, b, kb, qt, scores):
    count = chunks_of(s, z, b)
    q_block = group_row(s, z, b) * NZ + b

    def keep(c, size, high, x):
        scores[pl.ds(c, size)] = x.reshape(size, CK, QC)
        return jnp.maximum(high, jnp.max(x.reshape(size * CK // 8, 8, QC), axis=0))

    def score(c, size):
        return jnp.dot(rows_of(kb, c, size), qt[b], preferred_element_type=F32)

    def plain(c, size, high):
        return keep(c, size, high, score(c, size))

    def masked(c, size, high):
        row = lax.broadcasted_iota(jnp.int32, (size * CK, QC), 0)
        col = lax.broadcasted_iota(jnp.int32, (size * CK, QC), 1)
        key_pos = ((c * CB + row // T) * NZ + z) * T + row % T
        q_pos = q_block * T + col % T
        return keep(c, size, high, jnp.where(key_pos <= q_pos, score(c, size), LOW))

    odd = count % 2
    even = ((count > 0) & (odd == 0)).astype(jnp.int32)
    high = jnp.full((8, QC), LOW, F32)
    high = tiles(count - odd - 2 * even, plain, high)
    high = lax.fori_loop(0, even, lambda i, now: masked(count - 2, 2, now), high)
    high = lax.fori_loop(0, odd, lambda i, now: masked(count - 1, 1, now), high)
    return jnp.max(high, axis=0, keepdims=True) * C2


def prob_block(s, z, b, row_max, vt, scores, probs, out_t):
    base = base_of(s, z, b)
    out_t[b] = jnp.zeros((D, QC), F32)

    def step(c, size, total):
        p = jnp.exp2(scores[pl.ds(c, size)].reshape(size * CK, QC) * C2 - row_max)
        total = total + jnp.sum(p.reshape(size * CK // 8, 8, QC), axis=0)
        pb = p.astype(BF16)
        probs[pl.ds(base + c, size)] = pb.reshape(size, CK, QC)
        out_t[b] += jnp.dot(lanes_of(vt, c, size), pb, preferred_element_type=F32)
        return total

    total = tiles(chunks_of(s, z, b), step, jnp.zeros((8, QC), F32))
    return jnp.sum(total, axis=0, keepdims=True)


def by_head(row):
    parts = [row[:, h * T : (h + 1) * T] for h in range(HEADS)]
    return jnp.concatenate(parts + [jnp.zeros((8 - HEADS, T), F32)], axis=0)


def in_line(rows):
    return jnp.concatenate([rows[h : h + 1] for h in range(HEADS)], axis=1)


def stat_block(z, b, row_max, row_sum, gt, out_t, stats, top):
    part_delta = jnp.sum(gt[b].astype(F32) * out_t[b], axis=0, keepdims=True)
    row_sum = jnp.maximum(row_sum, 1e-37)
    top[b] = row_max
    stats[b, z, pl.ds(0, 8), :] = by_head(row_max + jnp.log2(row_sum))
    stats[b, z, pl.ds(8, 8), :] = by_head(part_delta / row_sum)
    stats[b, z, pl.ds(16, 8), :] = by_head(row_max)


def merge_stats(b, stats, top, coef, delta, parts):
    logs = [stats[b, j, pl.ds(0, 8), :] for j in range(NZ)]
    high = functools.reduce(jnp.maximum, logs)
    log_total = high + jnp.log2(sum(jnp.exp2(x - high) for x in logs))
    shares = [jnp.exp2(x - log_total) for x in logs]
    coef[b] = jnp.exp2(top[b] - in_line(log_total))
    if parts is not None:
        for j in range(NZ):
            parts[j] = in_line(jnp.exp2(stats[b, j, pl.ds(16, 8), :] - log_total))
    delta[b] = in_line(sum(stats[b, j, pl.ds(8, 8), :] * shares[j] for j in range(NZ)))


def backward_tile(s, z, b, c, size, vb, kt, qh, gh, gt, probs, coef, delta, dq_t, dkv):
    base = base_of(s, z, b)
    dw = jnp.dot(rows_of(vb, c, size), gt[b], preferred_element_type=F32)
    w = probs[pl.ds(base + c, size)].reshape(size * CK, QC).astype(F32) * coef[b]
    ds = (w * (dw - delta[b])).astype(BF16)
    wb = w.astype(BF16)
    rows = pl.ds(pl.multiple_of(c * CK, CK), size * CK)
    dkv[rows, pl.ds(0, D)] += jnp.dot(ds, qh[b], preferred_element_type=F32)
    dkv[rows, pl.ds(D, D)] += jnp.dot(wb, gh[b], preferred_element_type=F32)
    dq_t[b] += jnp.dot(lanes_of(kt, c, size), ds, preferred_element_type=F32)


def kernel(
    q_ref, k_ref, v_ref, g_ref,
    att_ref, gq_ref, gk_ref, gv_ref,
    kb, vb, kt, vt, qh, gh, qt, gt, scores, probs, out_t, dq_t, stats, top, coef, delta, dkv,
    sib_in, kv_out, kv_in, q_mid, g_mid, o_out, o_in, part_coef, dq_out, dq_in,
    k_send, k_recv, kf_send, v_send, v_recv, vf_send, q_send, q_recv, qm_recv, qp_send, g_send, g_recv, gm_recv, gp_send,
    st_send, st_recv, o_send, o_recv, dq_send, dq_recv, sib_send, sib_recv, dkv_send, dkv_recv,
):
    ia = lax.axis_index("ctxa")
    ib = lax.axis_index("ctxb")
    z = ib % NZ
    s = ia * 2 + ib // NZ
    core = ia % 2
    x = (ia // 2) % 4
    y = (ia // 8) * 2 + ib // NZ
    sibling = s + 2 - 4 * core
    mirror = NS - 1 - s
    chip = (s // 4) * 2 + s % 2

    def device(row, plane):
        return (row // 2, (row % 2) * NZ + plane)

    def remote(src, dst, send, recv, row, plane):
        return pltpu.make_async_remote_copy(
            src_ref=src, dst_ref=dst, send_sem=send, recv_sem=recv,
            device_id=device(row, plane), device_id_type=MESH,
        )

    def each(low, high, step):
        lax.fori_loop(low, high, lambda i, _: (step(i), 0)[1], 0)

    def moved(i, sign):
        nx = (x + sign * (i % 4) + 4) % 4
        ny = (y + sign * (i // 4) + 4) % 4
        return (ny // 2) * 16 + nx * 4 + core * 2 + ny % 2

    def member(i):
        b = (z + i) % NZ
        return b, group_row(s, z, b)

    barrier = pltpu.get_barrier_semaphore()

    def signal(row, plane):
        pl.semaphore_signal(
            barrier, inc=1, device_id=device(row, plane), device_id_type=MESH
        )

    each(1, NS // 2, lambda i: signal(moved(i, 1), z))
    signal(sibling, z)
    for i in range(1, NZ):
        b, row = member(i)
        signal(row, b)
    signal(mirror, z)
    signal(s, (z + 1) % NZ)
    signal(s, (z + 3) % NZ)

    kb[s] = k_ref[...]
    vb[s] = v_ref[...]
    for h in range(HEADS):
        qh[z, pl.ds(h * T, T), :] = q_ref[:, pl.ds(h * D, D)]
        gh[z, pl.ds(h * T, T), :] = g_ref[:, pl.ds(h * D, D)]

    pl.semaphore_wait(barrier, NS // 2 - 1 + 1 + NZ - 1 + 3)

    def k_copy(i):
        return remote(kb.at[s], kb.at[s], k_send.at[i], k_recv.at[s], moved(i, 1), z)

    def v_copy(i):
        return remote(vb.at[s], vb.at[s], v_send.at[i], v_recv.at[s], moved(i, 1), z)

    def q_copy(i):
        if i == 0:
            return remote(qh.at[z], q_mid, q_send.at[0], qm_recv, mirror, z)
        return remote(qh.at[z], qh.at[z], q_send.at[1], q_recv.at[z], s, (z + 2) % NZ)

    def g_copy(i):
        if i == 0:
            return remote(gh.at[z], g_mid, g_send.at[0], gm_recv, mirror, z)
        return remote(gh.at[z], gh.at[z], g_send.at[1], g_recv.at[z], s, (z + 2) % NZ)

    def q_pass(i):
        return remote(q_mid, qh.at[z], qp_send.at[i], q_recv.at[z], s, (z + 1 + 2 * i) % NZ)

    def g_pass(i):
        return remote(g_mid, gh.at[z], gp_send.at[i], g_recv.at[z], s, (z + 1 + 2 * i) % NZ)

    def k_pass(i):
        row = moved(i, -1)
        return remote(kb.at[row], kb.at[row], kf_send.at[i], k_recv.at[row], sibling, z)

    def v_pass(i):
        row = moved(i, -1)
        return remote(vb.at[row], vb.at[row], vf_send.at[i], v_recv.at[row], sibling, z)

    q_copy(0).start()
    q_copy(1).start()
    each(1, NS // 2, lambda i: k_copy(i).start())
    each(1, NS // 2, lambda i: v_copy(i).start())
    g_copy(0).start()
    g_copy(1).start()

    transpose_heads(qh, qt, z)
    transpose_heads(gh, gt, z)
    dkv[...] = jnp.zeros((NS * T, 2 * D), F32)
    dq_t[...] = jnp.zeros((NZ, D, QC), F32)

    def gather(buf, flipped, copy, send, recv, between):
        def wait(row):
            remote(buf.at[row], buf.at[row], send.at[0], recv.at[row], sibling, z).wait_recv()

        def near(i):
            row = moved(i, -1)

            @pl.when(i > 0)
            def _():
                wait(row)

            copy(i).start()
            transpose_rows(buf, flipped, row)

        def far(i):
            row = moved(i, -1) + 2 - 4 * core
            wait(row)
            transpose_rows(buf, flipped, row)

        each(0, NS // 2, near)
        between()
        each(0, NS // 2, far)

    def pass_q():
        q_copy(0).wait_recv()
        q_pass(0).start()
        q_pass(1).start()

    def pass_g():
        g_copy(0).wait_recv()
        g_pass(0).start()
        g_pass(1).start()

    gather(kb, kt, k_pass, k_send, k_recv, pass_q)

    def st_copy(b, i):
        p, row = member(i)
        return remote(stats.at[b, z], stats.at[b, z], st_send.at[b, i], st_recv.at[b, z], row, p)

    def o_copy(i):
        b, row = member(i)
        return remote(o_out.at[b], o_in.at[i - 1], o_send.at[i], o_recv.at[i - 1], row, b)

    def dq_copy(i):
        b, row = member(i)
        return remote(dq_out.at[b], dq_in.at[i - 1], dq_send.at[i], dq_recv.at[i - 1], row, b)

    def forward_step(i):
        b = (z + i + (i == 2).astype(jnp.int32) - (i == 3).astype(jnp.int32)) % NZ
        row = group_row(s, z, b)

        @pl.when(i > 0)
        def _():
            remote(qh.at[b], qh.at[b], q_send.at[0], q_recv.at[b], row, b).wait_recv()
            transpose_heads(qh, qt, b)

        row_max = score_block(s, z, b, kb, qt, scores)

        @pl.when(i == 0)
        def _():
            gather(vb, vt, v_pass, v_send, v_recv, pass_g)

        row_sum = prob_block(s, z, b, row_max, vt, scores, probs, out_t)

        @pl.when(i > 0)
        def _():
            o_out[b] = out_t[b].astype(BF16)
            remote(
                o_out.at[b], o_in.at[(b - z + NZ) % NZ - 1], o_send.at[(b - z + NZ) % NZ],
                o_recv.at[(b - z + NZ) % NZ - 1], row, b,
            ).start()
            remote(gh.at[b], gh.at[b], g_send.at[0], g_recv.at[b], row, b).wait_recv()
            transpose_heads(gh, gt, b)

        stat_block(z, b, row_max, row_sum, gt, out_t, stats, top)
        each(1, NZ, lambda j: st_copy(b, j).start())

    each(0, NZ, forward_step)

    def merge(b, parts=None):
        def wait(j):
            p, row = member(j)
            remote(
                stats.at[b, p], stats.at[b, p], st_send.at[b, 0], st_recv.at[b, p], row, p
            ).wait_recv()

        each(1, NZ, wait)
        merge_stats(b, stats, top, coef, delta, parts)

    def tile(b, c, size):
        backward_tile(s, z, b, c, size, vb, kt, qh, gh, gt, probs, coef, delta, dq_t, dkv)

    def send_dq(i):
        b = (z + i) % NZ
        dq_out[b] = dq_t[b].astype(BF16)
        dq_copy(i).start()

    for i in (1, 3):
        b = (z + i) % NZ
        merge(b)
        tiles(chunks_of(s, z, b), lambda c, size, now: (tile(b, c, size), now)[1], 0)
        send_dq(i)

    merge((z + 2) % NZ)
    merge(z, part_coef)

    def round_at(i):
        ny = (y // 2 + i // 4) % 2
        nx = (x + i % 4) % 4
        return ny * 4 + nx

    def core_rows(i, which):
        return pl.ds(pl.multiple_of(round_at(i) * 4 * T + which * 2 * T, 2 * T), 2 * T)

    def sib_copy(i):
        return remote(
            dkv.at[core_rows(i, 1 - core), :], sib_in.at[i], sib_send.at[i], sib_recv.at[i], sibling, z
        )

    def dkv_copy(i, j):
        row = round_at(i) * 4 + core * 2 + j
        return remote(
            kv_out.at[2 * i + j], kv_in.at[chip], dkv_send.at[2 * i + j], dkv_recv.at[chip], row, z
        )

    def finish(i):
        sib_copy(i).wait_recv()
        for j in range(2):
            rows = pl.ds(pl.multiple_of(round_at(i) * 4 * T + core * 2 * T + j * T, T), T)
            terms = dkv[rows, :] + sib_in[i, pl.ds(j * T, T), :]
            kv_out[2 * i + j, pl.ds(0, T), :] = (terms[:, :D] * SCALE).astype(BF16)
            kv_out[2 * i + j, pl.ds(T, T), :] = terms[:, D:].astype(BF16)
            mine = (i == 0) & (y % 2 == j)

            @pl.when(jnp.logical_not(mine))
            def _():
                dkv_copy(i, j).start()

            @pl.when(mine)
            def _():
                kv_in[chip] = kv_out[2 * i + j]

    def round_step(i):
        c = 2 * round_at(i)

        def one(j):
            b = (z + 2 * j) % NZ
            left = chunks_of(s, z, b) - c

            @pl.when(left > 1)
            def _():
                tile(b, c, 2)

            @pl.when(left == 1)
            def _():
                tile(b, c, 1)

        each(0, 2, one)
        sib_copy(i).start()

        @pl.when(i > 0)
        def _():
            finish(i - 1)

    each(0, ROUNDS, round_step)
    send_dq(2)
    finish(ROUNDS - 1)

    for i in range(1, NZ):
        o_copy(i).wait_recv()
    out_t[z] = out_t[z] * coef[z] + sum(
        o_in[i - 1].astype(F32) * part_coef[(z - i + NZ) % NZ] for i in range(1, NZ)
    )
    for h in range(HEADS):
        att_ref[:, pl.ds(h * D, D)] = out_t[z, :, pl.ds(h * T, T)].T.astype(BF16)

    for i in range(1, NZ):
        dq_copy(i).wait_recv()
    dq_t[z] = (dq_t[z] + sum(dq_in[i].astype(F32) for i in range(NZ - 1))) * SCALE
    for h in range(HEADS):
        gq_ref[:, pl.ds(h * D, D)] = dq_t[z, :, pl.ds(h * T, T)].T.astype(BF16)

    def wait_kv(i):
        row = (i // 2) * 4 + core * 2 + i % 2

        @pl.when(i != chip)
        def _():
            remote(kv_out.at[0], kv_in.at[i], dkv_send.at[0], dkv_recv.at[i], row, z).wait_recv()

    each(0, NS // 2, wait_kv)
    for part in range(4):
        rows = pl.ds(part * T // 4, T // 4)
        gk_ref[rows, :] = jnp.sum(kv_in[:, rows, :].astype(F32), axis=0).astype(BF16)
        rows = pl.ds(T + part * T // 4, T // 4)
        gv_ref[pl.ds(part * T // 4, T // 4), :] = jnp.sum(kv_in[:, rows, :].astype(F32), axis=0).astype(BF16)

    each(1, NS // 2, lambda i: k_copy(i).wait_send())
    each(1, NS // 2, lambda i: v_copy(i).wait_send())
    each(0, NS // 2, lambda i: k_pass(i).wait_send())
    each(0, NS // 2, lambda i: v_pass(i).wait_send())

    for i in range(2):
        q_copy(i).wait_send()
        g_copy(i).wait_send()
        q_pass(i).wait_send()
        g_pass(i).wait_send()
    for i in range(1, NZ):
        o_copy(i).wait_send()
        dq_copy(i).wait_send()
    each(0, NZ, lambda b: each(1, NZ, lambda j: st_copy(b, j).wait_send()))

    def drain_kv(i):
        sib_copy(i).wait_send()
        for j in range(2):

            @pl.when((i != 0) | (y % 2 != j))
            def _():
                dkv_copy(i, j).wait_send()

    each(0, ROUNDS, drain_kv)


def shards(queries, keys, values, grad_out):
    vmem = pl.BlockSpec(memory_space=pltpu.VMEM)
    dma = pltpu.SemaphoreType.DMA
    return pl.pallas_call(
        kernel,
        out_shape=(
            jax.ShapeDtypeStruct((T, QC), BF16),
            jax.ShapeDtypeStruct((T, QC), BF16),
            jax.ShapeDtypeStruct((T, D), BF16),
            jax.ShapeDtypeStruct((T, D), BF16),
        ),
        in_specs=[vmem] * 4,
        out_specs=(vmem,) * 4,
        scratch_shapes=[
            pltpu.VMEM((NS, T, D), BF16),
            pltpu.VMEM((NS, T, D), BF16),
            pltpu.VMEM((D, NS * T), BF16),
            pltpu.VMEM((D, NS * T), BF16),
            pltpu.VMEM((NZ, QC, D), BF16),
            pltpu.VMEM((NZ, QC, D), BF16),
            pltpu.VMEM((NZ, D, QC), BF16),
            pltpu.VMEM((NZ, D, QC), BF16),
            pltpu.VMEM((NCH, CK, QC), F32),
            pltpu.VMEM((MAXP, CK, QC), BF16),
            pltpu.VMEM((NZ, D, QC), F32),
            pltpu.VMEM((NZ, D, QC), F32),
            pltpu.VMEM((NZ, NZ, 24, T), F32),
            pltpu.VMEM((NZ, 1, QC), F32),
            pltpu.VMEM((NZ, 1, QC), F32),
            pltpu.VMEM((NZ, 1, QC), F32),
            pltpu.VMEM((NS * T, 2 * D), F32),
            pltpu.VMEM((ROUNDS, 2 * T, 2 * D), F32),
            pltpu.VMEM((NCH, 2 * T, D), BF16),
            pltpu.VMEM((NS // 2, 2 * T, D), BF16),
            pltpu.VMEM((QC, D), BF16),
            pltpu.VMEM((QC, D), BF16),
            pltpu.VMEM((NZ, D, QC), BF16),
            pltpu.VMEM((NZ - 1, D, QC), BF16),
            pltpu.VMEM((NZ, 1, QC), F32),
            pltpu.VMEM((NZ, D, QC), BF16),
            pltpu.VMEM((NZ - 1, D, QC), BF16),
            dma((NS // 2,)),
            dma((NS,)),
            dma((NS // 2,)),
            dma((NS // 2,)),
            dma((NS,)),
            dma((NS // 2,)),
            dma((2,)),
            dma((NZ,)),
            dma(()),
            dma((2,)),
            dma((2,)),
            dma((NZ,)),
            dma(()),
            dma((2,)),
            dma((NZ, NZ)),
            dma((NZ, NZ)),
            dma((NZ,)),
            dma((NZ - 1,)),
            dma((NZ,)),
            dma((NZ - 1,)),
            dma((ROUNDS,)),
            dma((ROUNDS,)),
            dma((NCH,)),
            dma((NS // 2,)),
        ],
        compiler_params=pltpu.CompilerParams(
            collective_id=0, has_side_effects=True, vmem_limit_bytes=60 * 1024 * 1024
        ),
        cost_estimate=pl.CostEstimate(
            flops=10_000_000_000, bytes_accessed=10_000_000, transcendentals=6_500_000
        ),
    )(queries, keys, values, grad_out)


def solution(mesh):
    spec = P(("ctxa", "ctxb"), None)
    return jax.shard_map(
        shards,
        mesh=mesh,
        in_specs=(spec,) * 4,
        out_specs=(spec,) * 4,
        check_vma=False,
    )
```

time: 104 us -> 92.4 us (0.89)
  Pallas kernels: 97.6 us -> 86.2 us
    pallas_call x1, Pallas kernels: 97.6 us -> 86.2 us  [shards(): pl.pallas_call(kernel, out_shape=(jax.ShapeDtypeStruct((T, QC), BF16), ja...]
where the time goes in v3:
time: 92.4 us; the launch traced here: 90.7 us
  Pallas kernels  86.2 us (93%)
  local copies, waits for them, and re-layouts  3.8 us (4%)
    pallas_call x1, Pallas kernels, shards(): pl.pallas_call(kernel, out_shape=(jax.ShapeDtypeStruct((T, QC), BF16), ja...  86.2 us
    unnamed x10, local copies, waits for them, and re-layouts  3.8 us

profile of v3, /device:TPU:0, one launch (start us, length us, event | category | flops | bytes accessed | tf_op | source)
XLA Modules:
  0.0 90.7 jit_solution(15572143799693173769)
XLA Ops:
  0.6 86.2 %shard_map.75 = (bf16[128,768]{1,0:T(8,128)(2,1)}, bf16[128,768]{1,0:T(8,128)(2,1)}, bf16[128,128]{1,0:T(8,128)(2,1)}, bf16[128,128]{1,0:T(8,128)(2,1)}) custom-call(bf16[128,768]{1,0:T(8,128)(2,1)} %q_ref.1, bf16[128,128]{1,0:T(8,128)(2,1)} %k_ref.1, bf16[128,128]{1,0:T(8,128)(2,1)} %v_ref.1, bf16[128,768]{1,0:T(8,128)(2,1)} %g_ref.1), custom_call_target="tpu_custom_call" | custom-call | flops 10000000000 | bytes 10000000 | tf_op jit(solution)/shard_map/pallas_call | solution.py:491
  86.9 0.0 copy-start
  86.9 1.7 %copy.12 = bf16[128,768]{1,0:T(8,128)(2,1)} copy(bf16[128,768]{1,0:T(8,128)(2,1)} %get-tuple-element.8) | data formatting | bytes 393216
  88.6 0.0 copy-done
  88.6 0.0 copy-start.2
  88.6 0.7 copy.13
  89.2 0.1 copy-done.2
  89.3 0.0 copy-start.1
  89.3 0.6 copy.14
  89.9 0.2 copy-done.1
  90.1 0.6 copy.15
Async XLA Ops:
  86.9 1.7 %copy-start = (bf16[128,768]{1,0:T(8,128)(2,1)S(1)}, bf16[128,768]{1,0:T(8,128)(2,1)}, u32[]{:S(2)}) copy-start(bf16[128,768]{1,0:T(8,128)(2,1)} %get-tuple-element.9) | copy-start | bytes 589828
  88.6 0.8 copy-start.2
  89.3 0.8 copy-start.1

commit v4 on v3

--- a/solution.py
+++ b/solution.py
@@ -124,10 +124,9 @@
     return jnp.concatenate([rows[h : h + 1] for h in range(HEADS)], axis=1)
 
 
-def stat_block(z, b, row_max, row_sum, gt, out_t, stats, top):
+def stat_block(z, b, row_max, row_sum, gt, out_t, stats):
     part_delta = jnp.sum(gt[b].astype(F32) * out_t[b], axis=0, keepdims=True)
     row_sum = jnp.maximum(row_sum, 1e-37)
-    top[b] = row_max
     stats[b, z, pl.ds(0, 8), :] = by_head(row_max + jnp.log2(row_sum))
     stats[b, z, pl.ds(8, 8), :] = by_head(part_delta / row_sum)
     stats[b, z, pl.ds(16, 8), :] = by_head(row_max)
@@ -160,7 +159,7 @@
 def kernel(
     q_ref, k_ref, v_ref, g_ref,
     att_ref, gq_ref, gk_ref, gv_ref,
-    kb, vb, kt, vt, qh, gh, qt, gt, scores, probs, out_t, dq_t, stats, top, coef, delta, dkv,
+    kb, vb, kt, vt, qh, gh, qt, gt, scores, probs, out_t, dq_t, stats, top, sums, coef, delta, dkv,
     sib_in, kv_out, kv_in, q_mid, g_mid, o_out, o_in, part_coef, dq_out, dq_in,
     k_send, k_recv, kf_send, v_send, v_recv, vf_send, q_send, q_recv, qm_recv, qp_send, g_send, g_recv, gm_recv, gp_send,
     st_send, st_recv, o_send, o_recv, dq_send, dq_recv, sib_send, sib_recv, dkv_send, dkv_recv,
@@ -311,7 +310,7 @@
         return remote(dq_out.at[b], dq_in.at[i - 1], dq_send.at[i], dq_recv.at[i - 1], row, b)
 
     def forward_step(i):
-        b = (z + i + (i == 2).astype(jnp.int32) - (i == 3).astype(jnp.int32)) % NZ
+        b = (z + i + (i == 1).astype(jnp.int32) - (i == 2).astype(jnp.int32)) % NZ
         row = group_row(s, z, b)
 
         @pl.when(i > 0)
@@ -319,28 +318,36 @@
             remote(qh.at[b], qh.at[b], q_send.at[0], q_recv.at[b], row, b).wait_recv()
             transpose_heads(qh, qt, b)
 
-        row_max = score_block(s, z, b, kb, qt, scores)
+        top[b] = score_block(s, z, b, kb, qt, scores)
 
         @pl.when(i == 0)
         def _():
             gather(vb, vt, v_pass, v_send, v_recv, pass_g)
 
-        row_sum = prob_block(s, z, b, row_max, vt, scores, probs, out_t)
+        sums[b] = prob_block(s, z, b, top[b], vt, scores, probs, out_t)
+
+    each(0, NZ, forward_step)
+
+    def stats_step(i):
+        b = (z + i + (i == 1).astype(jnp.int32) - (i == 2).astype(jnp.int32)) % NZ
+        row = group_row(s, z, b)
 
         @pl.when(i > 0)
         def _():
-            o_out[b] = out_t[b].astype(BF16)
-            remote(
-                o_out.at[b], o_in.at[(b - z + NZ) % NZ - 1], o_send.at[(b - z + NZ) % NZ],
-                o_recv.at[(b - z + NZ) % NZ - 1], row, b,
-            ).start()
             remote(gh.at[b], gh.at[b], g_send.at[0], g_recv.at[b], row, b).wait_recv()
             transpose_heads(gh, gt, b)
 
-        stat_block(z, b, row_max, row_sum, gt, out_t, stats, top)
+        stat_block(z, b, top[b], sums[b], gt, out_t, stats)
         each(1, NZ, lambda j: st_copy(b, j).start())
 
-    each(0, NZ, forward_step)
+    each(0, NZ, stats_step)
+
+    def send_o(i):
+        b, row = member(i)
+        o_out[b] = out_t[b].astype(BF16)
+        o_copy(i).start()
+
+    each(1, NZ, send_o)
 
     def merge(b, parts=None):
         def wait(j):
@@ -370,8 +377,9 @@
     merge(z, part_coef)
 
     def round_at(i):
-        ny = (y // 2 + i // 4) % 2
-        nx = (x + i % 4) % 4
+        k = i % 4
+        ny = (y // 2 + i + i // 4) % 2
+        nx = (x + k + (k == 2).astype(jnp.int32) - (k == 3).astype(jnp.int32)) % 4
         return ny * 4 + nx
 
     def core_rows(i, which):
@@ -423,13 +431,13 @@
         each(0, 2, one)
         sib_copy(i).start()
 
-        @pl.when(i > 0)
+        @pl.when(i > 1)
         def _():
-            finish(i - 1)
+            finish(i - 2)
 
     each(0, ROUNDS, round_step)
     send_dq(2)
-    finish(ROUNDS - 1)
+    each(ROUNDS - 2, ROUNDS, finish)
 
     for i in range(1, NZ):
         o_copy(i).wait_recv()
@@ -485,10 +493,15 @@
     each(0, ROUNDS, drain_kv)
 
 
+def hand_on(*refs):
+    for i in range(4):
+        refs[4 + i][...] = refs[i][...]
+
+
 def shards(queries, keys, values, grad_out):
     vmem = pl.BlockSpec(memory_space=pltpu.VMEM)
     dma = pltpu.SemaphoreType.DMA
-    return pl.pallas_call(
+    results = pl.pallas_call(
         kernel,
         out_shape=(
             jax.ShapeDtypeStruct((T, QC), BF16),
@@ -512,6 +525,7 @@
             pltpu.VMEM((NZ, D, QC), F32),
             pltpu.VMEM((NZ, D, QC), F32),
             pltpu.VMEM((NZ, NZ, 24, T), F32),
+            pltpu.VMEM((NZ, 1, QC), F32),
             pltpu.VMEM((NZ, 1, QC), F32),
             pltpu.VMEM((NZ, 1, QC), F32),
             pltpu.VMEM((NZ, 1, QC), F32),
@@ -558,6 +572,12 @@
             flops=10_000_000_000, bytes_accessed=10_000_000, transcendentals=6_500_000
         ),
     )(queries, keys, values, grad_out)
+    return pl.pallas_call(
+        hand_on,
+        out_shape=tuple(jax.ShapeDtypeStruct(r.shape, r.dtype) for r in results),
+        in_specs=[vmem] * 4,
+        out_specs=(vmem,) * 4,
+    )(*results)
 
 
 def solution(mesh):

time: 92.4 us -> 86.8 us (0.939)
  local copies, waits for them, and re-layouts: 3.8 us -> 0 us
    unnamed x10 -> x0, local copies, waits for them, and re-layouts: 3.8 us -> none
    pallas_call x1, Pallas kernels: 86.2 us -> 83.5 us  [shards(): pl.pallas_call(kernel, out_shape=(jax.ShapeDtypeStruct((T, QC), BF16), ja...]
    pallas_call x0 -> x1, Pallas kernels: none -> 1.8 us  [shards(): pl.pallas_call(hand_on, out_shape=tuple((jax.ShapeDtypeStruct(r.shape, r....]
where the time goes in v4:
time: 86.8 us; the launch traced here: 86 us
  Pallas kernels  85.3 us (98%)
    pallas_call x1, Pallas kernels, shards(): pl.pallas_call(kernel, out_shape=(jax.ShapeDtypeStruct((T, QC), BF16), ja...  83.5 us
    pallas_call x1, Pallas kernels, shards(): pl.pallas_call(hand_on, out_shape=tuple((jax.ShapeDtypeStruct(r.shape, r....  1.8 us

profile of v4, /device:TPU:0, one launch (start us, length us, event | category | flops | bytes accessed | tf_op | source)
XLA Modules:
  0.0 86.0 jit_solution(10431686626701581337)
XLA Ops:
  0.6 83.5 %shard_map.75 = (bf16[128,768]{1,0:T(8,128)(2,1)}, bf16[128,768]{1,0:T(8,128)(2,1)}, bf16[128,128]{1,0:T(8,128)(2,1)}, bf16[128,128]{1,0:T(8,128)(2,1)}) custom-call(bf16[128,768]{1,0:T(8,128)(2,1)} %q_ref.1, bf16[128,128]{1,0:T(8,128)(2,1)} %k_ref.1, bf16[128,128]{1,0:T(8,128)(2,1)} %v_ref.1, bf16[128,768]{1,0:T(8,128)(2,1)} %g_ref.1), custom_call_target="tpu_custom_call" | custom-call | flops 10000000000 | bytes 10000000 | tf_op jit(solution)/shard_map/pallas_call | solution.py:504
  84.2 1.8 %shard_map.76 = (bf16[128,768]{1,0:T(8,128)(2,1)}, bf16[128,768]{1,0:T(8,128)(2,1)}, bf16[128,128]{1,0:T(8,128)(2,1)}, bf16[128,128]{1,0:T(8,128)(2,1)}) custom-call(bf16[128,768]{1,0:T(8,128)(2,1)} %get-tuple-element.8.refs_0_, bf16[128,768]{1,0:T(8,128)(2,1)} %get-tuple-element.9.refs_1_, bf16[128,128]{1,0:T(8,128)(2,1)} %get-tuple-element.10.refs_2_, ...), custom_call_target="tpu_custom_call" | custom-call | tf_op jit(solution)/shard_map/pallas_call | solution.py:575

commit v5 on v4

--- a/solution.py
+++ b/solution.py
@@ -144,16 +144,19 @@
     delta[b] = in_line(sum(stats[b, j, pl.ds(8, 8), :] * shares[j] for j in range(NZ)))
 
 
-def backward_tile(s, z, b, c, size, vb, kt, qh, gh, gt, probs, coef, delta, dq_t, dkv):
-    base = base_of(s, z, b)
-    dw = jnp.dot(rows_of(vb, c, size), gt[b], preferred_element_type=F32)
-    w = probs[pl.ds(base + c, size)].reshape(size * CK, QC).astype(F32) * coef[b]
-    ds = (w * (dw - delta[b])).astype(BF16)
-    wb = w.astype(BF16)
+def backward_tile(s, z, blocks, c, size, vb, kt, qh, gh, gt, probs, coef, delta, dq_t, dkv):
+    key_sum, value_sum = 0.0, 0.0
+    for b in blocks:
+        base = base_of(s, z, b)
+        dw = jnp.dot(rows_of(vb, c, size), gt[b], preferred_element_type=F32)
+        w = probs[pl.ds(base + c, size)].reshape(size * CK, QC).astype(F32) * coef[b]
+        ds = (w * (dw - delta[b])).astype(BF16)
+        key_sum += jnp.dot(ds, qh[b], preferred_element_type=F32)
+        value_sum += jnp.dot(w.astype(BF16), gh[b], preferred_element_type=F32)
+        dq_t[b] += jnp.dot(lanes_of(kt, c, size), ds, preferred_element_type=F32)
     rows = pl.ds(pl.multiple_of(c * CK, CK), size * CK)
-    dkv[rows, pl.ds(0, D)] += jnp.dot(ds, qh[b], preferred_element_type=F32)
-    dkv[rows, pl.ds(D, D)] += jnp.dot(wb, gh[b], preferred_element_type=F32)
-    dq_t[b] += jnp.dot(lanes_of(kt, c, size), ds, preferred_element_type=F32)
+    dkv[rows, pl.ds(0, D)] += key_sum
+    dkv[rows, pl.ds(D, D)] += value_sum
 
 
 def kernel(
@@ -162,7 +165,8 @@
     kb, vb, kt, vt, qh, gh, qt, gt, scores, probs, out_t, dq_t, stats, top, sums, coef, delta, dkv,
     sib_in, kv_out, kv_in, q_mid, g_mid, o_out, o_in, part_coef, dq_out, dq_in,
     k_send, k_recv, kf_send, v_send, v_recv, vf_send, q_send, q_recv, qm_recv, qp_send, g_send, g_recv, gm_recv, gp_send,
-    st_send, st_recv, o_send, o_recv, dq_send, dq_recv, sib_send, sib_recv, dkv_send, dkv_recv,
+    st_send, st_recv, o_send, o_recv, dq_send, dq_recv, sib_send, sib_recv, dkv_send, dkv_recv, load_sem, store_sem,
+    att_rows, gq_rows, gk_rows, gv_rows,
 ):
     ia = lax.axis_index("ctxa")
     ib = lax.axis_index("ctxb")
@@ -212,11 +216,20 @@
     signal(s, (z + 1) % NZ)
     signal(s, (z + 3) % NZ)
 
-    kb[s] = k_ref[...]
-    vb[s] = v_ref[...]
+    loads = [
+        pltpu.make_async_copy(k_ref, kb.at[s], load_sem.at[0]),
+        pltpu.make_async_copy(v_ref, vb.at[s], load_sem.at[1]),
+    ]
     for h in range(HEADS):
-        qh[z, pl.ds(h * T, T), :] = q_ref[:, pl.ds(h * D, D)]
-        gh[z, pl.ds(h * T, T), :] = g_ref[:, pl.ds(h * D, D)]
+        lanes, rows = pl.ds(h * D, D), pl.ds(h * T, T)
+        loads.append(pltpu.make_async_copy(q_ref.at[:, lanes], qh.at[z, rows, :], load_sem.at[2 + h]))
+        loads.append(
+            pltpu.make_async_copy(g_ref.at[:, lanes], gh.at[z, rows, :], load_sem.at[2 + HEADS + h])
+        )
+    for load in loads:
+        load.start()
+    for load in loads:
+        load.wait()
 
     pl.semaphore_wait(barrier, NS // 2 - 1 + 1 + NZ - 1 + 3)
 
@@ -359,8 +372,8 @@
         each(1, NZ, wait)
         merge_stats(b, stats, top, coef, delta, parts)
 
-    def tile(b, c, size):
-        backward_tile(s, z, b, c, size, vb, kt, qh, gh, gt, probs, coef, delta, dq_t, dkv)
+    def tile(blocks, c, size):
+        backward_tile(s, z, blocks, c, size, vb, kt, qh, gh, gt, probs, coef, delta, dq_t, dkv)
 
     def send_dq(i):
         b = (z + i) % NZ
@@ -370,7 +383,7 @@
     for i in (1, 3):
         b = (z + i) % NZ
         merge(b)
-        tiles(chunks_of(s, z, b), lambda c, size, now: (tile(b, c, size), now)[1], 0)
+        tiles(chunks_of(s, z, b), lambda c, size, now: (tile((b,), c, size), now)[1], 0)
         send_dq(i)
 
     merge((z + 2) % NZ)
@@ -416,17 +429,25 @@
     def round_step(i):
         c = 2 * round_at(i)
 
+        pair = (z, (z + 2) % NZ)
+        left = [chunks_of(s, z, b) - c for b in pair]
+        whole = (left[0] > 1) & (left[1] > 1)
+
+        @pl.when(whole)
+        def _():
+            tile(pair, c, 2)
+
         def one(j):
             b = (z + 2 * j) % NZ
-            left = chunks_of(s, z, b) - c
-
-            @pl.when(left > 1)
+            rest = chunks_of(s, z, b) - c
+
+            @pl.when((rest > 1) & jnp.logical_not(whole))
             def _():
-                tile(b, c, 2)
-
-            @pl.when(left == 1)
+                tile((b,), c, 2)
+
+            @pl.when(rest == 1)
             def _():
-                tile(b, c, 1)
+                tile((b,), c, 1)
 
         each(0, 2, one)
         sib_copy(i).start()
@@ -445,27 +466,9 @@
         o_in[i - 1].astype(F32) * part_coef[(z - i + NZ) % NZ] for i in range(1, NZ)
     )
     for h in range(HEADS):
-        att_ref[:, pl.ds(h * D, D)] = out_t[z, :, pl.ds(h * T, T)].T.astype(BF16)
-
-    for i in range(1, NZ):
-        dq_copy(i).wait_recv()
-    dq_t[z] = (dq_t[z] + sum(dq_in[i].astype(F32) for i in range(NZ - 1))) * SCALE
-    for h in range(HEADS):
-        gq_ref[:, pl.ds(h * D, D)] = dq_t[z, :, pl.ds(h * T, T)].T.astype(BF16)
-
-    def wait_kv(i):
-        row = (i // 2) * 4 + core * 2 + i % 2
-
-        @pl.when(i != chip)
-        def _():
-            remote(kv_out.at[0], kv_in.at[i], dkv_send.at[0], dkv_recv.at[i], row, z).wait_recv()
-
-    each(0, NS // 2, wait_kv)
-    for part in range(4):
-        rows = pl.ds(part * T // 4, T // 4)
-        gk_ref[rows, :] = jnp.sum(kv_in[:, rows, :].astype(F32), axis=0).astype(BF16)
-        rows = pl.ds(T + part * T // 4, T // 4)
-        gv_ref[pl.ds(part * T // 4, T // 4), :] = jnp.sum(kv_in[:, rows, :].astype(F32), axis=0).astype(BF16)
+        att_rows[:, pl.ds(h * D, D)] = out_t[z, :, pl.ds(h * T, T)].T.astype(BF16)
+    att_store = pltpu.make_async_copy(att_rows, att_ref, store_sem.at[0])
+    att_store.start()
 
     each(1, NS // 2, lambda i: k_copy(i).wait_send())
     each(1, NS // 2, lambda i: v_copy(i).wait_send())
@@ -479,8 +482,16 @@
         g_pass(i).wait_send()
     for i in range(1, NZ):
         o_copy(i).wait_send()
-        dq_copy(i).wait_send()
     each(0, NZ, lambda b: each(1, NZ, lambda j: st_copy(b, j).wait_send()))
+
+
+    for i in range(1, NZ):
+        dq_copy(i).wait_recv()
+    dq_t[z] = (dq_t[z] + sum(dq_in[i].astype(F32) for i in range(NZ - 1))) * SCALE
+    for h in range(HEADS):
+        gq_rows[:, pl.ds(h * D, D)] = dq_t[z, :, pl.ds(h * T, T)].T.astype(BF16)
+    gq_store = pltpu.make_async_copy(gq_rows, gq_ref, store_sem.at[1])
+    gq_store.start()
 
     def drain_kv(i):
         sib_copy(i).wait_send()
@@ -491,6 +502,30 @@
                 dkv_copy(i, j).wait_send()
 
     each(0, ROUNDS, drain_kv)
+    for i in range(1, NZ):
+        dq_copy(i).wait_send()
+
+    def wait_kv(i):
+        row = (i // 2) * 4 + core * 2 + i % 2
+
+        @pl.when(i != chip)
+        def _():
+            remote(kv_out.at[0], kv_in.at[i], dkv_send.at[0], dkv_recv.at[i], row, z).wait_recv()
+
+    each(0, NS // 2, wait_kv)
+    for part in range(4):
+        rows = pl.ds(part * T // 4, T // 4)
+        gk_rows[rows, :] = jnp.sum(kv_in[:, rows, :].astype(F32), axis=0).astype(BF16)
+        rows = pl.ds(T + part * T // 4, T // 4)
+        gv_rows[pl.ds(part * T // 4, T // 4), :] = jnp.sum(kv_in[:, rows, :].astype(F32), axis=0).astype(BF16)
+    gk_store = pltpu.make_async_copy(gk_rows, gk_ref, store_sem.at[2])
+    gv_store = pltpu.make_async_copy(gv_rows, gv_ref, store_sem.at[3])
+    gk_store.start()
+    gv_store.start()
+    att_store.wait()
+    gq_store.wait()
+    gk_store.wait()
+    gv_store.wait()
 
 
 def hand_on(*refs):
@@ -499,6 +534,7 @@
 
 
 def shards(queries, keys, values, grad_out):
+    whole = pl.BlockSpec(memory_space=pl.ANY)
     vmem = pl.BlockSpec(memory_space=pltpu.VMEM)
     dma = pltpu.SemaphoreType.DMA
     results = pl.pallas_call(
@@ -509,8 +545,8 @@
             jax.ShapeDtypeStruct((T, D), BF16),
             jax.ShapeDtypeStruct((T, D), BF16),
         ),
-        in_specs=[vmem] * 4,
-        out_specs=(vmem,) * 4,
+        in_specs=[whole] * 4,
+        out_specs=(whole,) * 4,
         scratch_shapes=[
             pltpu.VMEM((NS, T, D), BF16),
             pltpu.VMEM((NS, T, D), BF16),
@@ -564,6 +600,12 @@
             dma((ROUNDS,)),
             dma((NCH,)),
             dma((NS // 2,)),
+            dma((2 + 2 * HEADS,)),
+            dma((4,)),
+            pltpu.VMEM((T, QC), BF16),
+            pltpu.VMEM((T, QC), BF16),
+            pltpu.VMEM((T, D), BF16),
+            pltpu.VMEM((T, D), BF16),
         ],
         compiler_params=pltpu.CompilerParams(
             collective_id=0, has_side_effects=True, vmem_limit_bytes=60 * 1024 * 1024

time: 86.8 us -> 85.8 us (0.988)
    pallas_call x1, Pallas kernels: 83.5 us -> 82.7 us  [shards(): pl.pallas_call(kernel, out_shape=(jax.ShapeDtypeStruct((T, QC), BF16), ja...]
where the time goes in v5:
time: 85.8 us; the launch traced here: 85.1 us
  Pallas kernels  84.5 us (98%)
    pallas_call x1, Pallas kernels, shards(): pl.pallas_call(kernel, out_shape=(jax.ShapeDtypeStruct((T, QC), BF16), ja...  82.7 us
    pallas_call x1, Pallas kernels, shards(): pl.pallas_call(hand_on, out_shape=tuple((jax.ShapeDtypeStruct(r.shape, r....  1.8 us

profile of v5, /device:TPU:0, one launch (start us, length us, event | category | flops | bytes accessed | tf_op | source)
XLA Modules:
  0.0 85.1 jit_solution(7521014382883195085)
XLA Ops:
  0.6 82.7 %shard_map.75 = (bf16[128,768]{1,0:T(8,128)(2,1)}, bf16[128,768]{1,0:T(8,128)(2,1)}, bf16[128,128]{1,0:T(8,128)(2,1)}, bf16[128,128]{1,0:T(8,128)(2,1)}) custom-call(bf16[128,768]{1,0:T(8,128)(2,1)} %q_ref.1, bf16[128,128]{1,0:T(8,128)(2,1)} %k_ref.1, bf16[128,128]{1,0:T(8,128)(2,1)} %v_ref.1, bf16[128,768]{1,0:T(8,128)(2,1)} %g_ref.1), custom_call_target="tpu_custom_call" | custom-call | flops 10000000000 | bytes 10000000 | tf_op jit(solution)/shard_map/pallas_call | solution.py:540
  83.3 1.8 %shard_map.76 = (bf16[128,768]{1,0:T(8,128)(2,1)}, bf16[128,768]{1,0:T(8,128)(2,1)}, bf16[128,128]{1,0:T(8,128)(2,1)}, bf16[128,128]{1,0:T(8,128)(2,1)}) custom-call(bf16[128,768]{1,0:T(8,128)(2,1)} %get-tuple-element.8.refs_0_, bf16[128,768]{1,0:T(8,128)(2,1)} %get-tuple-element.9.refs_1_, bf16[128,128]{1,0:T(8,128)(2,1)} %get-tuple-element.10.refs_2_, ...), custom_call_target="tpu_custom_call" | custom-call | tf_op jit(solution)/shard_map/pallas_call | solution.py:617

commit v6 on v5

--- a/solution.py
+++ b/solution.py
@@ -322,6 +322,11 @@
         b, row = member(i)
         return remote(dq_out.at[b], dq_in.at[i - 1], dq_send.at[i], dq_recv.at[i - 1], row, b)
 
+    def send_o(i):
+        b, row = member(i)
+        o_out[b] = out_t[b].astype(BF16)
+        o_copy(i).start()
+
     def forward_step(i):
         b = (z + i + (i == 1).astype(jnp.int32) - (i == 2).astype(jnp.int32)) % NZ
         row = group_row(s, z, b)
@@ -339,6 +344,10 @@
 
         sums[b] = prob_block(s, z, b, top[b], vt, scores, probs, out_t)
 
+        @pl.when(i > 0)
+        def _():
+            send_o((b - z + NZ) % NZ)
+
     each(0, NZ, forward_step)
 
     def stats_step(i):
@@ -354,13 +363,6 @@
         each(1, NZ, lambda j: st_copy(b, j).start())
 
     each(0, NZ, stats_step)
-
-    def send_o(i):
-        b, row = member(i)
-        o_out[b] = out_t[b].astype(BF16)
-        o_copy(i).start()
-
-    each(1, NZ, send_o)
 
     def merge(b, parts=None):
         def wait(j):

time: 85.8 us -> 94 us (1.096)
  Pallas kernels: 84.5 us -> 91.8 us
    pallas_call x1, Pallas kernels: 82.7 us -> 90 us  [shards(): pl.pallas_call(kernel, out_shape=(jax.ShapeDtypeStruct((T, QC), BF16), ja...]
where the time goes in v6:
time: 94 us; the launch traced here: 92.4 us
  Pallas kernels  91.8 us (98%)
    pallas_call x1, Pallas kernels, shards(): pl.pallas_call(kernel, out_shape=(jax.ShapeDtypeStruct((T, QC), BF16), ja...  90 us

profile of v6, /device:TPU:0, one launch (start us, length us, event | category | flops | bytes accessed | tf_op | source)
XLA Modules:
  0.0 92.4 jit_solution(3559492303593650479)
XLA Ops:
  0.6 90.0 %shard_map.75 = (bf16[128,768]{1,0:T(8,128)(2,1)}, bf16[128,768]{1,0:T(8,128)(2,1)}, bf16[128,128]{1,0:T(8,128)(2,1)}, bf16[128,128]{1,0:T(8,128)(2,1)}) custom-call(bf16[128,768]{1,0:T(8,128)(2,1)} %q_ref.1, bf16[128,128]{1,0:T(8,128)(2,1)} %k_ref.1, bf16[128,128]{1,0:T(8,128)(2,1)} %v_ref.1, bf16[128,768]{1,0:T(8,128)(2,1)} %g_ref.1), custom_call_target="tpu_custom_call" | custom-call | flops 10000000000 | bytes 10000000 | tf_op jit(solution)/shard_map/pallas_call | solution.py:542
  90.6 1.8 %shard_map.76 = (bf16[128,768]{1,0:T(8,128)(2,1)}, bf16[128,768]{1,0:T(8,128)(2,1)}, bf16[128,128]{1,0:T(8,128)(2,1)}, bf16[128,128]{1,0:T(8,128)(2,1)}) custom-call(bf16[128,768]{1,0:T(8,128)(2,1)} %get-tuple-element.8.refs_0_, bf16[128,768]{1,0:T(8,128)(2,1)} %get-tuple-element.9.refs_1_, bf16[128,128]{1,0:T(8,128)(2,1)} %get-tuple-element.10.refs_2_, ...), custom_call_target="tpu_custom_call" | custom-call | tf_op jit(solution)/shard_map/pallas_call | solution.py:619
